TPU v7x, 32 devices: a whole 2x2x4 slice. The times are simulated.
32 devices in a mesh: mode: 4 (over y, x), mer: 8 (over z, core).
Axes of the slice: x: 2, y: 2, z: 4, core: 2. Of those that a mesh axis runs over, the one named last changes fastest.
Arguments:
- field: float32 [32, 6, 4096], P('mode', None, 'mer'), may hold values from -6 to 6
- velocity: bfloat16 [3, 64, 4096], P(None, None, ('mer', 'mode')), may hold values from -4 to 4
- stiffness: float32 [64, 64], replicated, may hold values from -0.75 to 0.75
- curl_matrix: float32 [64, 64], replicated, may hold values from -0.75 to 0.75
- mass: float32 [4096], P('mer'), may hold values from 0.5 to 2
- connect: int32 [128, 64], P('mer'), may hold values from 0 to 767
- wall_index: int32 [512], P('mer'), may hold values from 0 to 511, as said below
- dtn: bfloat16 [32, 512, 512], P('mode', 'mer'), as said below
Outputs:
- advanced: float32 [32, 6, 4096], P('mode', None, 'mer')
- wall_flux: float32 [2, 32, 2, 512], P(None, 'mode', None, 'mer')
Inputs may be any that keep to these rules, and one draw needn't show every extreme that they name: `wall_index`: within each block of 64 consecutive entries the numbers are distinct. `dtn`: each mode's matrix is symmetric.
All inputs are finite; a program needn't handle non-finite values.
Results may differ from a plain program's by a relative error of at most 0.005.
Values may be sent and summed in bfloat16 or wider, within the bound.
A program may use at most 64 MiB of HBM per device.

v0:
```python
import jax
import jax.numpy as jnp
from jax import lax
from jax.sharding import PartitionSpec as P

GHOST = 256


HI = lax.Precision.HIGHEST


def from_behind(block, axis, distance):
    devices = range(lax.axis_size(axis))
    route = [(i - distance, i) for i in devices if i - distance in devices]
    return lax.ppermute(block, axis, route)


def tables(modes, nphi):
    m = jnp.arange(modes, dtype=jnp.float32)
    k = jnp.arange(nphi, dtype=jnp.float32)
    angle = 2.0 * jnp.pi * m[:, None] * k[None, :] / nphi
    forward = jnp.stack([jnp.cos(angle), -jnp.sin(angle)], 1)
    return (forward, forward / nphi)


def induced(moved, velocity):
    modes = moved.shape[0]
    nphi = velocity.shape[1]
    forward, inverse = tables(modes, nphi)
    phys = jnp.einsum("mpcn,mpk->ckn", moved.reshape(modes, 2, 3, -1), forward, precision=HI)
    vel = velocity.astype(jnp.float32)
    cross = jnp.stack(
        [
            vel[1] * phys[2] - vel[2] * phys[1],
            vel[2] * phys[0] - vel[0] * phys[2],
            vel[0] * phys[1] - vel[1] * phys[0],
        ]
    )
    back = jnp.einsum("ckn,mpk->mpcn", cross, inverse, precision=HI)
    return back.reshape(modes, 6, -1)


def split_pair(values):
    upper = values.astype(jnp.bfloat16)
    lower = (values - upper.astype(jnp.float32)).astype(jnp.bfloat16)
    return (upper, lower)


def element_sweep(extended, stiffness, curl_matrix, connect):
    mode_dev = extended.shape[0]
    ext_len = extended.shape[2]
    elem_dev = connect.shape[0]
    npe = connect.shape[1]
    per_block = min(elem_dev, max(1, 512 // npe))
    blocks = elem_dev // per_block
    rows = extended.reshape(mode_dev * 12, ext_len)
    rows_hi, rows_lo = split_pair(rows)
    indices = connect.reshape(blocks, per_block * npe)
    columns = jnp.arange(ext_len, dtype=jnp.int32)

    def step(summed, idx):
        onehot = (idx[:, None] == columns[None, :]).astype(jnp.bfloat16)
        picked = lax.dot_general(
            rows_hi, onehot, (((1,), (1,)), ((), ())), preferred_element_type=jnp.float32
        )
        picked = picked + lax.dot_general(
            rows_lo, onehot, (((1,), (1,)), ((), ())), preferred_element_type=jnp.float32
        )
        picked = picked.reshape(mode_dev, 12, per_block, npe)
        fvals = picked[:, :6]
        evals = picked[:, 6:].reshape(mode_dev, 2, 3, per_block, npe)
        evals = jnp.roll(evals, 1, axis=2).reshape(mode_dev, 6, per_block, npe)
        local = -1.0 * jnp.einsum("pq,maeq->maep", stiffness, fvals, precision=HI)
        local = local + jnp.einsum("pq,maeq->maep", curl_matrix, evals, precision=HI)
        flat = local.reshape(mode_dev * 6, per_block * npe)
        loc_hi, loc_lo = split_pair(flat)
        summed = summed + jnp.dot(loc_hi, onehot, preferred_element_type=jnp.float32)
        summed = summed + jnp.dot(loc_lo, onehot, preferred_element_type=jnp.float32)
        return (summed, None)

    start = jnp.zeros((mode_dev * 6, ext_len), jnp.float32)
    summed, unused = lax.scan(step, start, indices)
    return summed.reshape(mode_dev, 6, ext_len)


def rate(field, velocity, stiffness, curl_matrix, mass, connect, wall_index, dtn):
    mode_dev = field.shape[0]
    nodes_dev = field.shape[2]
    extra = GHOST
    field_far = from_behind(field[:, :, :extra], "mer", -1)
    moved = lax.all_to_all(field, "mode", split_axis=2, concat_axis=0, tiled=True)
    back = induced(moved, velocity)
    emf = lax.all_to_all(back, "mode", split_axis=0, concat_axis=2, tiled=True)
    emf_far = from_behind(emf[:, :, :extra], "mer", -1)
    far = jnp.concatenate([field_far, emf_far], 1)
    extended = jnp.concatenate([jnp.concatenate([field, emf], 1), far], 2)
    summed = element_sweep(extended, stiffness, curl_matrix, connect)
    incoming = from_behind(summed[:, :, nodes_dev:], "mer", 1)
    assembled = summed[:, :, :nodes_dev].at[:, :, :extra].add(incoming)
    trace = field[:, jnp.array([2, 5])][:, :, wall_index].astype(jnp.bfloat16)
    whole = lax.all_gather(trace, "mer", axis=2, tiled=True)
    flux = jnp.einsum("mwv,mpv->mpw", dtn, whole, preferred_element_type=jnp.float32)
    mode_num = lax.axis_index("mode") * mode_dev + jnp.arange(mode_dev, dtype=jnp.int32)
    coef = (mode_num.astype(jnp.float32) / all_modes(velocity)) ** 2
    total = assembled - 4.0 * coef[:, None, None] * mass[None, None, :] * field
    total = total.at[:, 2, wall_index].add(-0.5 * flux[:, 0])
    total = total.at[:, 5, wall_index].add(-0.5 * flux[:, 1])
    return (total / mass[None, None, :], flux)


def all_modes(velocity):
    return velocity.shape[1] // 2


def body(field, velocity, stiffness, curl_matrix, mass, connect, wall_index, dtn):
    args = (velocity, stiffness, curl_matrix, mass, connect, wall_index, dtn)
    first, flux_one = rate(field, *args)
    section = field + 0.2 * first
    second, flux_two = rate(section, *args)
    return (0.5 * (field + section + 0.2 * second), jnp.stack([flux_one, flux_two]))


def solution(mesh):
    placed = (
        P("mode", None, "mer"),
        P(None, None, ("mer", "mode")),
        P(),
        P(),
        P("mer"),
        P("mer", None),
        P("mer"),
        P("mode", "mer", None),
    )
    return jax.shard_map(
        body,
        mesh=mesh,
        in_specs=placed,
        out_specs=(P("mode", None, "mer"), P(None, "mode", None, "mer")),
        check_vma=False,
    )
```

profile of v0, /device:TPU:0, one launch (start us, length us, event | category | flops | bytes accessed | tf_op | source)
XLA Modules:
  0.0 125.9 jit_solution(6367745785083146236)
XLA Ops:
  0.6 1.7 %copy.140 = f32[8,6,512]{0,1,2:T(8,128)S(1)} copy(f32[8,6,512]{2,0,1:T(8,128)} %param.18) | data formatting | bytes 196608 | tf_op args[0]
  2.4 1.3 %reshape.321 = f32[4,1,6144]{2,1,0:T(1,128)} reshape(f32[512,6,8]{2,1,0:T(8,128)S(1)} %bitcast.196) | data formatting | bytes 196608
  3.8 5.2 %all-to-all-start = ((f32[4,1,6144]{2,1,0:T(1,128)}), f32[4,1,6144]{2,1,0:T(1,128)S(1)}, u32[]{:S(2)}, u32[]{:S(2)}) async-start(f32[4,1,6144]{2,1,0:T(1,128)} %reshape.321), calls=%async_computation | async-start | bytes 196608 | tf_op jit(solution)/shard_map/all_to_all | solution.py:91
  8.9 0.6 slice.160
  9.5 1.3 %collective-permute-start = (f32[8,6,256]{2,0,1:T(8,128)}, f32[8,6,256]{2,0,1:T(8,128)}, u32[]{:S(2)}, u32[]{:S(2)}) collective-permute-start(f32[8,6,256]{2,0,1:T(8,128)} %slice.160), channel_id=1, source_target_pairs={{1,0},{2,1},{3,2},{4,3},{5,4},{6,5},{7,6},{9,8},{10,9},{11,10},{12... | collective-permute-start | bytes 147464 | tf_op jit(solution)/shard_map/ppermute | solution.py:15
  11.1 0.6 gather_fusion
  11.8 0.6 gather_fusion.1
  12.5 15.7 %all_gather.6 = bf16[8,2,512]{0,1,2:T(2,128)(2,1)S(1)} all-gather(bf16[8,2,64]{0,1,2:T(2,128)(2,1)S(1)} %bitcast.219), channel_id=1, replica_groups=mesh['mode'=4,'mer'=8] {'mer'}, dimensions={2}, use_global_device_ids=true | all-gather | bytes 18432 | tf_op jit(solution)/shard_map/all_gather | solution.py:101
  28.6 0.5 broadcast.377
  29.2 0.9 reduce.4
  30.1 0.9 reshape.322
  31.0 0.5 copy.141
  32.1 0.7 copy.143
  32.8 4.3 %all-to-all-start.1 = ((f32[32,6,128]{2,1,0:T(8,128)}), f32[32,6,128]{2,1,0:T(8,128)S(1)}, u32[]{:S(2)}, u32[]{:S(2)}) async-start(f32[32,6,128]{2,1,0:T(8,128)} %copy.143), calls=%async_computation.1 | async-start | bytes 262144 | tf_op jit(solution)/shard_map/all_to_all | solution.py:93
  37.2 4.9 %all-to-all-done.1 = f32[32,6,128]{2,1,0:T(8,128)S(1)} async-done(((f32[32,6,128]{2,1,0:T(8,128)}), f32[32,6,128]{2,1,0:T(8,128)S(1)}, u32[]{:S(2)}, u32[]{:S(2)}) %all-to-all-start.1) | async-done | bytes 98336 | tf_op jit(solution)/shard_map/all_to_all | solution.py:93
  42.2 1.3 %collective-permute-start.1 = (f32[8,6,256]{2,0,1:T(8,128)S(1)}, f32[8,6,256]{2,0,1:T(8,128)S(1)}, u32[]{:S(2)}, u32[]{:S(2)}) collective-permute-start(f32[8,6,256]{2,0,1:T(8,128)S(1)} %slice.213), channel_id=1, source_target_pairs={{1,0},{2,1},{3,2},{4,3},{5,4},{6,5},{7,6},{9,8},{10,9},{11,10},{12... | collective-permute-start | bytes 147464 | tf_op jit(solution)/shard_map/ppermute | solution.py:15
  43.6 1.7 %collective-permute-done.1 = f32[8,6,256]{2,0,1:T(8,128)S(1)} collective-permute-done((f32[8,6,256]{2,0,1:T(8,128)S(1)}, f32[8,6,256]{2,0,1:T(8,128)S(1)}, u32[]{:S(2)}, u32[]{:S(2)}) %collective-permute-start.1) | collective-permute-done | bytes 49184 | tf_op jit(solution)/shard_map/ppermute | solution.py:15
  45.3 0.8 maximum_maximum_fusion
  46.3 5.9 %while.24 = (s32[]{:T(128)}, f32[48,768]{1,0:T(8,128)S(1)}, s32[2,512]{1,0:T(2,128)S(1)}, bf16[96,768]{1,0:T(8,128)(2,1)S(1)}, bf16[96,768]{1,0:T(8,128)(2,1)S(1...) while((s32[]{:T(128)}, f32[48,768]{1,0:T(8,128)S(1)}, ...), condition=%wide.region_1.2_spmd.clone, body=%wide.region_0.1_spmd.clone.sunk | while | flops 266170368 | bytes 3485803 | solution.py:82
  46.3 0.5 fusion.118
  46.9 0.5 fusion.119
  48.3 0.5 fusion.122
  48.8 0.5 fusion.123
  49.3 0.5 fusion.118
  49.8 0.5 fusion.119
  51.3 0.5 fusion.122
  51.8 0.5 fusion.123
  52.3 3.7 %collective-permute-start.2 = (f32[8,6,256]{2,0,1:T(8,128)S(1)}, f32[8,6,256]{2,0,1:T(8,128)S(1)}, u32[]{:S(2)}, u32[]{:S(2)}) collective-permute-start(f32[8,6,256]{2,0,1:T(8,128)S(1)} %copy.148), channel_id=1, source_target_pairs={{0,1},{1,2},{2,3},{3,4},{4,5},{5,6},{6,7},{8,9},{9,10},{10,11},{11... | collective-permute-start | bytes 147464 | tf_op jit(solution)/shard_map/ppermute | solution.py:15
  56.3 0.6 collective-permute-done.2
  57.0 0.5 copy.151
  57.4 3.7 %scatter_fusion = f32[8,6,512]{0,2,1:T(8,128)S(1)} fusion(f32[8,6,512]{0,2,1:T(8,128)S(1)} %copy.151, s32[64]{0:T(128)S(1)} %select_bitcast_fusion.1, f32[64,8]{1,0:T(8,128)S(1)} %copy.152), kind=kCustom, calls=%fused_computation.4 | custom fusion | flops 512 | bytes 6656 | tf_op jit(solution)/shard_map/scatter-add | solution.py:106
  61.2 3.7 %scatter_fusion.1 = f32[8,6,512]{0,2,1:T(8,128)S(1)} fusion(f32[8,6,512]{0,2,1:T(8,128)S(1)} %scatter_fusion, s32[64]{0:T(128)S(1)} %get-tuple-element.204, f32[64,8]{1,0:T(8,128)S(1)} %copy.153), kind=kCustom, calls=%fused_computation.5 | custom fusion | flops 512 | bytes 6656 | tf_op jit(solution)/shard_map/scatter-add | solution.py:107
  64.9 0.4 copy.154
  65.4 0.7 copy.155
  66.1 1.3 %reshape.323 = f32[4,1,6144]{2,1,0:T(1,128)} reshape(f32[512,6,8]{2,1,0:T(8,128)S(1)} %bitcast.197) | data formatting | bytes 196608
  67.4 3.3 %all-to-all-start.2 = ((f32[4,1,6144]{2,1,0:T(1,128)}), f32[4,1,6144]{2,1,0:T(1,128)S(1)}, u32[]{:S(2)}, u32[]{:S(2)}) async-start(f32[4,1,6144]{2,1,0:T(1,128)} %reshape.323), calls=%async_computation.2 | async-start | bytes 196608 | tf_op jit(solution)/shard_map/all_to_all | solution.py:91
  70.8 0.6 gather_fusion.2
  71.3 1.3 %collective-permute-start.3 = (f32[8,6,256]{2,0,1:T(8,128)S(1)}, f32[8,6,256]{2,0,1:T(8,128)S(1)}, u32[]{:S(2)}, u32[]{:S(2)}) collective-permute-start(f32[8,6,256]{2,0,1:T(8,128)S(1)} %slice.222), channel_id=1, source_target_pairs={{1,0},{2,1},{3,2},{4,3},{5,4},{6,5},{7,6},{9,8},{10,9},{11,10},{12... | collective-permute-start | bytes 147464 | tf_op jit(solution)/shard_map/ppermute | solution.py:15
  72.8 0.6 gather_fusion.3
  73.5 16.1 %all_gather.7 = bf16[8,2,512]{0,1,2:T(2,128)(2,1)S(1)} all-gather(bf16[8,2,64]{0,1,2:T(2,128)(2,1)S(1)} %bitcast.218), channel_id=1, replica_groups=mesh['mode'=4,'mer'=8] {'mer'}, dimensions={2}, use_global_device_ids=true | all-gather | bytes 18432 | tf_op jit(solution)/shard_map/all_gather | solution.py:101
  89.7 0.9 reduce.5
  90.6 0.9 reshape.324
  91.4 0.5 copy.156
  92.6 0.7 copy.158
  93.3 4.1 %all-to-all-start.3 = ((f32[32,6,128]{2,1,0:T(8,128)}), f32[32,6,128]{2,1,0:T(8,128)S(1)}, u32[]{:S(2)}, u32[]{:S(2)}) async-start(f32[32,6,128]{2,1,0:T(8,128)} %copy.158), calls=%async_computation.3 | async-start | bytes 262144 | tf_op jit(solution)/shard_map/all_to_all | solution.py:93
  97.7 4.8 %all-to-all-done.3 = f32[32,6,128]{2,1,0:T(8,128)S(1)} async-done(((f32[32,6,128]{2,1,0:T(8,128)}), f32[32,6,128]{2,1,0:T(8,128)S(1)}, u32[]{:S(2)}, u32[]{:S(2)}) %all-to-all-start.3) | async-done | bytes 98336 | tf_op jit(solution)/shard_map/all_to_all | solution.py:93
  102.5 1.3 %collective-permute-start.4 = (f32[8,6,256]{2,0,1:T(8,128)S(1)}, f32[8,6,256]{2,0,1:T(8,128)S(1)}, u32[]{:S(2)}, u32[]{:S(2)}) collective-permute-start(f32[8,6,256]{2,0,1:T(8,128)S(1)} %slice.223), channel_id=1, source_target_pairs={{1,0},{2,1},{3,2},{4,3},{5,4},{6,5},{7,6},{9,8},{10,9},{11,10},{12... | collective-permute-start | bytes 147464 | tf_op jit(solution)/shard_map/ppermute | solution.py:15
  103.8 1.8 %collective-permute-done.4 = f32[8,6,256]{2,0,1:T(8,128)S(1)} collective-permute-done((f32[8,6,256]{2,0,1:T(8,128)S(1)}, f32[8,6,256]{2,0,1:T(8,128)S(1)}, u32[]{:S(2)}, u32[]{:S(2)}) %collective-permute-start.4) | collective-permute-done | bytes 49184 | tf_op jit(solution)/shard_map/ppermute | solution.py:15
  105.8 5.9 %while.25 = (s32[]{:T(128)}, f32[48,768]{1,0:T(8,128)S(1)}, s32[2,512]{1,0:T(2,128)S(1)}, bf16[96,768]{1,0:T(8,128)(2,1)S(1)}, bf16[96,768]{1,0:T(8,128)(2,1)S(1...) while((s32[]{:T(128)}, f32[48,768]{1,0:T(8,128)S(1)}, ...), condition=%wide.region_5.6_spmd.clone, body=%wide.region_4.5_spmd.clone.sunk | while | flops 266170368 | bytes 3485803 | solution.py:82
  105.9 0.5 fusion.131
  106.4 0.5 fusion.132
  107.8 0.5 fusion.135
  108.3 0.5 fusion.136
  108.8 0.5 fusion.131
  109.3 0.5 fusion.132
  110.8 0.5 fusion.135
  111.3 0.5 fusion.136
  111.8 4.1 %collective-permute-start.5 = (f32[8,6,256]{2,0,1:T(8,128)S(1)}, f32[8,6,256]{2,0,1:T(8,128)S(1)}, u32[]{:S(2)}, u32[]{:S(2)}) collective-permute-start(f32[8,6,256]{2,0,1:T(8,128)S(1)} %copy.163), channel_id=1, source_target_pairs={{0,1},{1,2},{2,3},{3,4},{4,5},{5,6},{6,7},{8,9},{9,10},{10,11},{11... | collective-permute-start | bytes 147464 | tf_op jit(solution)/shard_map/ppermute | solution.py:15
  116.0 0.6 pad_maximum_fusion.3
  116.9 0.5 copy.166
  117.4 3.7 %scatter_fusion.2 = f32[8,6,512]{0,2,1:T(8,128)S(1)} fusion(f32[8,6,512]{0,2,1:T(8,128)S(1)} %copy.166, s32[64]{0:T(128)S(1)} %select_bitcast_fusion.1, f32[64,8]{1,0:T(8,128)S(1)} %copy.167), kind=kCustom, calls=%fused_computation.6 | custom fusion | flops 512 | bytes 6656 | tf_op jit(solution)/shard_map/scatter-add | solution.py:106
  121.1 3.7 %scatter_fusion.3 = f32[8,6,512]{0,2,1:T(8,128)S(1)} fusion(f32[8,6,512]{0,2,1:T(8,128)S(1)} %scatter_fusion.2, s32[64]{0:T(128)S(1)} %get-tuple-element.204, f32[64,8]{1,0:T(8,128)S(1)} %copy.168), kind=kCustom, calls=%fused_computation.7 | custom fusion | flops 512 | bytes 6656 | tf_op jit(solution)/shard_map/scatter-add | solution.py:107
  124.8 0.4 copy.169
  125.2 0.7 add_multiply_fusion
  (122 shorter events, 7.3 us)
Async XLA Ops:
  0.6 27.7 %copy-start = (bf16[8,64,512]{2,1,0:T(8,128)(2,1)S(1)}, bf16[8,64,512]{2,1,0:T(8,128)(2,1)}, u32[]{:S(2)}) copy-start(bf16[8,64,512]{2,1,0:T(8,128)(2,1)} %param.25) | copy-start | bytes 1572868
  2.4 6.6 %copy-start.3 = (f32[8,6,512]{2,0,1:T(8,128)S(1)}, f32[8,6,512]{2,0,1:T(8,128)}, u32[]{:S(2)}) copy-start(f32[8,6,512]{2,0,1:T(8,128)} %param.18) | copy-start | bytes 294916
  2.4 8.6 %copy-start.7 = (bf16[3,64,128]{2,1,0:T(8,128)(2,1)S(1)}, bf16[3,64,128]{2,1,0:T(8,128)(2,1)}, u32[]{:S(2)}) copy-start(bf16[3,64,128]{2,1,0:T(8,128)(2,1)} %param.19) | copy-start | bytes 147460
  2.4 8.6 %copy-start.11 = (s32[64]{0:T(128)S(1)}, s32[64]{0:T(128)}, u32[]{:S(2)}) copy-start(s32[64]{0:T(128)} %param.24) | copy-start | bytes 772
  2.4 8.7 %copy-start.10 = (s32[2]{0:T(128)S(1)}, s32[2]{0:T(128)}, u32[]{:S(2)}) copy-start(s32[2]{0:T(128)} %constant.180) | copy-start | bytes 28
  3.8 24.9 %all-to-all-start = ((f32[4,1,6144]{2,1,0:T(1,128)}), f32[4,1,6144]{2,1,0:T(1,128)S(1)}, u32[]{:S(2)}, u32[]{:S(2)}) async-start(f32[4,1,6144]{2,1,0:T(1,128)} %reshape.321), calls=%async_computation | async-start | bytes 196608 | tf_op jit(solution)/shard_map/all_to_all | solution.py:91
  9.5 34.0 %collective-permute-start = (f32[8,6,256]{2,0,1:T(8,128)}, f32[8,6,256]{2,0,1:T(8,128)}, u32[]{:S(2)}, u32[]{:S(2)}) collective-permute-start(f32[8,6,256]{2,0,1:T(8,128)} %slice.160), channel_id=1, source_target_pairs={{1,0},{2,1},{3,2},{4,3},{5,4},{6,5},{7,6},{9,8},{10,9},{11,10},{12... | collective-permute-start | bytes 147464 | tf_op jit(solution)/shard_map/ppermute | solution.py:15
  11.0 20.8 %copy-start.4 = (f32[3,64,128]{2,1,0:T(8,128)}, f32[3,64,128]{2,1,0:T(8,128)S(1)}, u32[]{:S(2)}) copy-start(f32[3,64,128]{2,1,0:T(8,128)S(1)} %convert_element_type.56) | copy-start | bytes 294916
  30.9 6.2 %copy-start.8 = (f32[512]{0:T(512)S(1)}, f32[512]{0:T(512)}, u32[]{:S(2)}) copy-start(f32[512]{0:T(512)} %param.22) | copy-start | bytes 6148
  30.9 12.5 %copy-start.9 = (s32[16,64]{1,0:T(8,128)S(1)}, s32[16,64]{1,0:T(8,128)}, u32[]{:S(2)}) copy-start(s32[16,64]{1,0:T(8,128)} %param.23) | copy-start | bytes 12292
  32.8 13.5 %copy-start.1 = (f32[64,64]{1,0:T(8,128)S(1)}, f32[64,64]{1,0:T(8,128)}, u32[]{:S(2)}) copy-start(f32[64,64]{1,0:T(8,128)} %param.20) | copy-start | bytes 49156
  32.8 13.5 %copy-start.2 = (f32[64,64]{1,0:T(8,128)S(1)}, f32[64,64]{1,0:T(8,128)}, u32[]{:S(2)}) copy-start(f32[64,64]{1,0:T(8,128)} %param.21) | copy-start | bytes 49156
  32.8 9.3 %all-to-all-start.1 = ((f32[32,6,128]{2,1,0:T(8,128)}), f32[32,6,128]{2,1,0:T(8,128)S(1)}, u32[]{:S(2)}, u32[]{:S(2)}) async-start(f32[32,6,128]{2,1,0:T(8,128)} %copy.143), calls=%async_computation.1 | async-start | bytes 262144 | tf_op jit(solution)/shard_map/all_to_all | solution.py:93
  42.2 3.1 %collective-permute-start.1 = (f32[8,6,256]{2,0,1:T(8,128)S(1)}, f32[8,6,256]{2,0,1:T(8,128)S(1)}, u32[]{:S(2)}, u32[]{:S(2)}) collective-permute-start(f32[8,6,256]{2,0,1:T(8,128)S(1)} %slice.213), channel_id=1, source_target_pairs={{1,0},{2,1},{3,2},{4,3},{5,4},{6,5},{7,6},{9,8},{10,9},{11,10},{12... | collective-permute-start | bytes 147464 | tf_op jit(solution)/shard_map/ppermute | solution.py:15
  52.3 4.6 %collective-permute-start.2 = (f32[8,6,256]{2,0,1:T(8,128)S(1)}, f32[8,6,256]{2,0,1:T(8,128)S(1)}, u32[]{:S(2)}, u32[]{:S(2)}) collective-permute-start(f32[8,6,256]{2,0,1:T(8,128)S(1)} %copy.148), channel_id=1, source_target_pairs={{0,1},{1,2},{2,3},{3,4},{4,5},{5,6},{6,7},{8,9},{9,10},{10,11},{11... | collective-permute-start | bytes 147464 | tf_op jit(solution)/shard_map/ppermute | solution.py:15
  67.4 22.2 %all-to-all-start.2 = ((f32[4,1,6144]{2,1,0:T(1,128)}), f32[4,1,6144]{2,1,0:T(1,128)S(1)}, u32[]{:S(2)}, u32[]{:S(2)}) async-start(f32[4,1,6144]{2,1,0:T(1,128)} %reshape.323), calls=%async_computation.2 | async-start | bytes 196608 | tf_op jit(solution)/shard_map/all_to_all | solution.py:91
  71.3 32.5 %collective-permute-start.3 = (f32[8,6,256]{2,0,1:T(8,128)S(1)}, f32[8,6,256]{2,0,1:T(8,128)S(1)}, u32[]{:S(2)}, u32[]{:S(2)}) collective-permute-start(f32[8,6,256]{2,0,1:T(8,128)S(1)} %slice.222), channel_id=1, source_target_pairs={{1,0},{2,1},{3,2},{4,3},{5,4},{6,5},{7,6},{9,8},{10,9},{11,10},{12... | collective-permute-start | bytes 147464 | tf_op jit(solution)/shard_map/ppermute | solution.py:15
  91.4 0.9 copy-start.5
  93.3 9.2 %all-to-all-start.3 = ((f32[32,6,128]{2,1,0:T(8,128)}), f32[32,6,128]{2,1,0:T(8,128)S(1)}, u32[]{:S(2)}, u32[]{:S(2)}) async-start(f32[32,6,128]{2,1,0:T(8,128)} %copy.158), calls=%async_computation.3 | async-start | bytes 262144 | tf_op jit(solution)/shard_map/all_to_all | solution.py:93
  97.7 8.2 %copy-start.6 = (f32[48,768]{1,0:T(8,128)S(1)}, f32[48,768]{1,0:T(8,128)}, u32[]{:S(2)}) copy-start(f32[48,768]{1,0:T(8,128)} %custom-call.9) | copy-start | bytes 442372
  102.5 3.1 %collective-permute-start.4 = (f32[8,6,256]{2,0,1:T(8,128)S(1)}, f32[8,6,256]{2,0,1:T(8,128)S(1)}, u32[]{:S(2)}, u32[]{:S(2)}) collective-permute-start(f32[8,6,256]{2,0,1:T(8,128)S(1)} %slice.223), channel_id=1, source_target_pairs={{1,0},{2,1},{3,2},{4,3},{5,4},{6,5},{7,6},{9,8},{10,9},{11,10},{12... | collective-permute-start | bytes 147464 | tf_op jit(solution)/shard_map/ppermute | solution.py:15
  111.8 5.0 %collective-permute-start.5 = (f32[8,6,256]{2,0,1:T(8,128)S(1)}, f32[8,6,256]{2,0,1:T(8,128)S(1)}, u32[]{:S(2)}, u32[]{:S(2)}) collective-permute-start(f32[8,6,256]{2,0,1:T(8,128)S(1)} %copy.163), channel_id=1, source_target_pairs={{0,1},{1,2},{2,3},{3,4},{4,5},{5,6},{6,7},{8,9},{9,10},{10,11},{11... | collective-permute-start | bytes 147464 | tf_op jit(solution)/shard_map/ppermute | solution.py:15
where the time goes:
time: 127 us; the launch traced here: 126 us
  blocking collectives  31.8 us (25%)
  starting transfers between devices  29.9 us (24%)
  other arithmetic  19.3 us (15%)
  local copies, waits for them, and re-layouts  17.5 us (14%)
  waiting for transfers between devices  13.9 us (11%)
  matrix products  11.8 us (9%)
  between operations  1.31 us (1%)
    all_gather x2, blocking collectives, rate(): whole = lax.all_gather(trace, 'mer', axis=2, tiled=True)  31.8 us
    ppermute x6, starting transfers between devices, from_behind(): return lax.ppermute(block, axis, route)  13 us
    all_to_all x2, waiting for transfers between devices, rate(): emf = lax.all_to_all(back, 'mode', split_axis=0, concat_axis=2, tiled=True)  9.74 us
    all_to_all x2, starting transfers between devices, rate(): lax.all_to_all(field, 'mode', split_axis=2, concat_axis=0, tiled=True)  8.47 us
    all_to_all x2, starting transfers between devices, rate(): emf = lax.all_to_all(back, 'mode', split_axis=0, concat_axis=2, tiled=True)  8.47 us
    scatter-add x2, other arithmetic, rate(): total = total.at[:, 2, wall_index].add(-0.5 * flux[:, 0])  7.43 us
    scatter-add x2, other arithmetic, rate(): total = total.at[:, 5, wall_index].add(-0.5 * flux[:, 1])  7.43 us
    unnamed x31, local copies, waits for them, and re-layouts  6.36 us
  transfers between devices with their start and end apart: 10, of which 5 were waited for; matrix products, arithmetic and copies ran while one was open for 11% of the time, Pallas kernels for 0%

commit v1 on v0

v1 whole, which is shorter than its diff:
```python
import functools

import jax
import jax.numpy as jnp
import numpy as np
from jax import lax
from jax.experimental import pallas as pl
from jax.experimental.pallas import tpu as pltpu
from jax.sharding import PartitionSpec as P

GHOST = 256
PAD = 8
MESH = pl.DeviceIdType.MESH
BF = jnp.bfloat16
F32 = jnp.float32


def transforms(modes, nphi):
    angle = 2.0 * np.pi * ((np.arange(modes)[:, None] * np.arange(nphi)[None, :]) % nphi) / nphi
    table = np.stack([np.cos(angle), -np.sin(angle)], 1)
    forward = np.zeros((3, nphi, modes, PAD))
    inverse = np.zeros((modes, PAD, 3, nphi))
    for p in range(2):
        for c in range(3):
            forward[c, :, :, 3 * p + c] = table[:, p].T
            inverse[:, 3 * p + c, (c - 1) % 3, :] = table[:, p] / nphi
    forward = forward.reshape(3 * nphi, modes * PAD)
    inverse = inverse.reshape(modes * PAD, 3 * nphi)
    return jnp.asarray(forward, BF), jnp.asarray(inverse, BF)


def mm(a, b):
    return jnp.dot(a, b, preferred_element_type=F32)


def mm_t(a, b):
    return lax.dot_general(a, b, (((1,), (1,)), ((), ())), preferred_element_type=F32)


def onehot(hit):
    return jnp.where(hit, 1.0, 0.0).astype(BF)


def iota(shape, dim):
    return lax.broadcasted_iota(jnp.int32, shape, dim)


def kernel(
    n_mode,
    n_mer,
    modes,
    field_ref,
    vel_ref,
    stiff_ref,
    curl_ref,
    mass_ref,
    connect_ref,
    wall_ref,
    dtn_ref,
    forward_ref,
    inverse_ref,
    out_ref,
    flux_ref,
    f_full,
    f_part,
    f_got,
    f_prev,
    f_next,
    e_part,
    e_own,
    e_prev,
    e_next,
    t_part,
    t_got,
    c_prev,
    kmat,
    pick,
    oper,
    wall_hot,
    send_sem,
    recv_sem,
):
    mode_dev, _, nodes = field_ref.shape
    nphi = vel_ref.shape[1]
    rows = mode_dev * PAD
    chunk = nodes // n_mode
    ghosts = GHOST // chunk
    elems, npe = connect_ref.shape
    wall_dev = wall_ref.shape[1]
    slots = elems * npe
    ext = nodes + GHOST
    me = lax.axis_index("mode")
    d = lax.axis_index("mer")
    has_prev = d > 0
    has_next = d < n_mer - 1

    def at(mode, mer):
        return {"mode": mode, "mer": mer}

    def other_mode(k):
        return lax.rem(me + k, n_mode)

    def other_mer(k):
        return lax.rem(d + k, n_mer)

    barrier = pltpu.get_barrier_semaphore()

    def greet(mode, mer):
        pl.semaphore_signal(barrier, inc=1, device_id=at(mode, mer), device_id_type=MESH)

    for k in range(1, n_mode):
        greet(other_mode(k), d)

    @pl.when(has_prev)
    def _():
        for k in range(n_mode):
            greet(other_mode(k), d - 1)

    @pl.when(has_next)
    def _():
        for k in range(n_mode):
            greet(other_mode(k), d + 1)

    for k in range(1, n_mer):
        peer = other_mer(k)

        @pl.when(jnp.logical_and(peer != d - 1, peer != d + 1))
        def _():
            greet(me, peer)

    s_f = 0
    s_eo = s_f + n_mode
    s_ep = s_eo + n_mode
    s_en = s_ep + n_mode
    s_fp = s_en + n_mode
    s_fn = s_fp + 1
    s_t = s_fn + 1
    s_c = s_t + n_mer

    def copy(src, dst, sec, out_no, in_no, mode, mer):
        return pltpu.make_async_remote_copy(
            src_ref=src,
            dst_ref=dst,
            send_sem=send_sem.at[sec, out_no],
            recv_sem=recv_sem.at[sec, in_no],
            device_id=at(mode, mer),
            device_id_type=MESH,
        )

    def f_copies(sec):
        return [
            copy(f_part.at[sec, other_mode(k)], f_got.at[sec, me], sec, s_f + other_mode(k), s_f + me, other_mode(k), d)
            for k in range(1, n_mode)
        ]

    def t_copies(sec):
        return [
            copy(t_part.at[sec], t_got.at[sec, d], sec, s_t + other_mer(k), s_t + d, me, other_mer(k))
            for k in range(1, n_mer)
        ]

    def up_copies(sec):
        made = [copy(f_full.at[sec], f_prev.at[sec], sec, s_fp, s_fp, me, d + 1)]
        if sec == 0:
            made.append(copy(connect_ref, c_prev, sec, s_c, s_c, me, d + 1))
        return made

    def down_copies(sec):
        return [copy(f_full.at[sec, :, pl.ds(0, GHOST)], f_next.at[sec], sec, s_fn, s_fn, me, d - 1)]

    def e_copies(sec):
        return [
            copy(e_part.at[sec, other_mode(k)], e_own.at[sec, me], sec, s_eo + other_mode(k), s_eo + me, other_mode(k), d)
            for k in range(1, n_mode)
        ]

    def e_up_copies(sec):
        return [
            copy(e_part.at[sec, other_mode(k)], e_prev.at[sec, me], sec, s_ep + other_mode(k), s_ep + me, other_mode(k), d + 1)
            for k in range(n_mode)
        ]

    def e_down_copies(sec):
        return [
            copy(e_part.at[sec, other_mode(k)], e_next.at[sec, me], sec, s_en + other_mode(k), s_en + me, other_mode(k), d - 1)
            for k in range(n_mode)
        ]

    sends_down = jnp.logical_and(has_prev, me < ghosts)

    def start(copies):
        for c in copies:
            c.start()

    def sent(copies):
        for c in copies:
            c.wait_send()

    def arrive(ref, sec, no):
        copy(ref, ref, sec, no, no, me, d).wait_recv()

    field = jnp.concatenate(
        [
            part
            for m in range(mode_dev)
            for part in (field_ref[m], jnp.zeros((PAD - 6, nodes), F32))
        ],
        0,
    )
    halves = 128 // wall_dev
    wall_row = jnp.concatenate([wall_ref[...]] * halves, 1)
    lane = iota((1, 128), 1)
    wall_row = jnp.where(lane // wall_dev == lax.rem(d, halves), wall_row, -1)
    wall_hot[...] = onehot(iota((nodes, 128), 0) == wall_row)

    take_row = iota((2 * mode_dev, rows), 0)
    take = onehot(iota((2 * mode_dev, rows), 1) == (take_row // 2) * PAD + 2 + 3 * (take_row % 2))
    put_row = iota((rows, 2 * mode_dev), 1)
    put = onehot(iota((rows, 2 * mode_dev), 0) == (put_row // 2) * PAD + 2 + 3 * (put_row % 2))

    def stage(sec, value):
        low = value.astype(BF)
        f_full[sec] = low
        for j in range(n_mode):
            f_part[sec, j] = low[:, j * chunk : (j + 1) * chunk]
        f_got[sec, me] = f_part[sec, me]

    def stage_trace(sec):
        walls = mm(mm(take, f_full[sec]).astype(BF), wall_hot[...]).astype(BF)
        t_part[sec] = walls
        t_got[sec, d] = walls

    def send_field(sec):
        start(f_copies(sec))

        @pl.when(has_next)
        def _():
            start(up_copies(sec))

        @pl.when(has_prev)
        def _():
            start(down_copies(sec))

    stage(0, field)

    @pl.when(jnp.logical_not(has_prev))
    def _():
        f_prev[...] = jnp.zeros(f_prev.shape, BF)
        e_prev[...] = jnp.zeros(e_prev.shape, BF)
        c_prev[...] = jnp.full(c_prev.shape, -1, jnp.int32)

    @pl.when(jnp.logical_not(has_next))
    def _():
        f_next[...] = jnp.zeros(f_next.shape, BF)
        e_next[...] = jnp.zeros(e_next.shape, BF)

    prev_n = has_prev.astype(jnp.int32)
    next_n = has_next.astype(jnp.int32)
    pl.semaphore_wait(barrier, n_mode - 1 + n_mer - 1 + (n_mode - 1) * (prev_n + next_n))

    send_field(0)
    stage_trace(0)
    start(t_copies(0))

    group = 256 // npe
    same = iota((256, 256), 0) // npe == iota((256, 256), 1) // npe

    def spread(ref, sign):
        wide = jnp.concatenate([sign * ref[...]] * group, 1)
        return jnp.where(same, jnp.concatenate([wide] * group, 0), 0.0).astype(BF)

    kmat[0] = spread(stiff_ref, -1.0)
    kmat[1] = spread(curl_ref, 1.0)
    blocks = nodes // 256
    step = 128

    def fill_pick(ref):
        numbers = jnp.concatenate([ref[e : e + 1, :] for e in range(elems)], 1)

        def fill(i, carry):
            base = pl.multiple_of(i * step, step)
            pick[pl.ds(base, step), :] = onehot(iota((step, slots), 0) + base == numbers)
            return carry

        lax.fori_loop(0, ext // step, fill, 0)

    def build(index, first, which):
        take_rows = pick[pl.ds(pl.multiple_of(first, 256), 256), :]
        moved = jnp.concatenate(
            [mm(take_rows[:, g * 256 : (g + 1) * 256], kmat[which]).astype(BF) for g in range(slots // 256)], 1
        )
        oper[index] = mm_t(pick[...], moved).astype(BF)

    def build_own(i, carry):
        build(i, lax.rem(i, blocks) * 256, i // blocks)
        return carry

    def build_prev(i, carry):
        build(2 * blocks + i, nodes, i)
        return carry

    fill_pick(connect_ref)
    lax.fori_loop(0, 2 * blocks, build_own, 0)

    mass_inv = 1.0 / mass_ref[...]
    mode_no = me * mode_dev + iota((rows, 1), 0) // PAD
    damp = 4.0 * (mode_no.astype(F32) / modes) ** 2

    def apply(own, nxt, prv, which):
        here = jnp.concatenate([own, nxt], 1)
        sums = [mm(here, oper[which * blocks + b]) for b in range(blocks)]
        sums[0] = sums[0] + mm(jnp.concatenate([prv, own[:, :GHOST]], 1), oper[2 * blocks + which])
        return jnp.concatenate(sums, 1)

    def lanes(ref, sec, count):
        return jnp.concatenate([ref[sec, j] for j in range(count)], 1)

    def rate(sec, value):
        for k in range(1, n_mode):
            arrive(f_got.at[sec, other_mode(k)], sec, s_f + other_mode(k))
        phys = mm(forward_ref[...], f_got[sec].reshape(n_mode * rows, chunk))
        px, py, pz = [phys[c * nphi : (c + 1) * nphi] for c in range(3)]
        vx, vy, vz = [vel_ref[c].astype(F32) for c in range(3)]
        cross = jnp.concatenate([vy * pz - vz * py, vz * px - vx * pz, vx * py - vy * px], 0)
        emf = mm(inverse_ref[...], cross.astype(BF)).astype(BF)
        e_part[sec] = emf.reshape(n_mode, rows, chunk)
        e_own[sec, me] = e_part[sec, me]
        start(e_copies(sec))

        @pl.when(has_next)
        def _():
            start(e_up_copies(sec))

        @pl.when(sends_down)
        def _():
            start(e_down_copies(sec))

        if sec == 0:

            @pl.when(has_prev)
            def _():
                arrive(c_prev, sec, s_c)

            fill_pick(c_prev)
            lax.fori_loop(0, 2, build_prev, 0)

        @pl.when(has_prev)
        def _():
            arrive(f_prev.at[sec], sec, s_fp)

        @pl.when(has_next)
        def _():
            arrive(f_next.at[sec], sec, s_fn)

        total = apply(f_full[sec], f_next[sec], f_prev[sec], 0)

        for k in range(1, n_mer):
            arrive(t_got.at[sec, other_mer(k)], sec, s_t + other_mer(k))
        trace = jnp.concatenate(
            [sum([t_got[sec, i + h] for h in range(1, halves)], t_got[sec, i]) for i in range(0, n_mer, halves)], 1
        )
        wide = mm_t(trace, dtn_ref[...].reshape(mode_dev * wall_dev, trace.shape[1]))
        wide = jnp.where(iota(wide.shape, 1) // wall_dev == iota(wide.shape, 0) // 2, wide, 0.0)
        folded = sum([wide[:, i : i + 128] for i in range(128, wide.shape[1], 128)], wide[:, :128])
        flux = sum([folded[:, h * wall_dev : (h + 1) * wall_dev] for h in range(1, halves)], folded[:, :wall_dev])
        for m in range(mode_dev):
            flux_ref[sec, m] = flux[2 * m : 2 * m + 2]
        spots = mm_t(jnp.concatenate([-0.5 * flux] * halves, 1).astype(BF), wall_hot[...])
        total = total + mm(put, spots.astype(BF))

        for k in range(1, n_mode):
            arrive(e_own.at[sec, other_mode(k)], sec, s_eo + other_mode(k))

        @pl.when(has_prev)
        def _():
            for j in range(n_mode):
                arrive(e_prev.at[sec, j], sec, s_ep + j)

        @pl.when(has_next)
        def _():
            for j in range(ghosts):
                arrive(e_next.at[sec, j], sec, s_en + j)

        total = total + apply(lanes(e_own, sec, n_mode), lanes(e_next, sec, ghosts), lanes(e_prev, sec, n_mode), 1)
        return total * mass_inv - damp * value

    section = field + 0.2 * rate(0, field)
    stage(1, section)
    send_field(1)
    stage_trace(1)
    start(t_copies(1))
    second = rate(1, section)
    advanced = 0.5 * (field + section + 0.2 * second)
    for m in range(mode_dev):
        out_ref[m] = advanced[m * PAD : m * PAD + 6]

    for sec in range(2):
        sent(f_copies(sec))
        sent(t_copies(sec))
        sent(e_copies(sec))

        @pl.when(has_next)
        def _():
            sent(up_copies(sec))
            sent(e_up_copies(sec))

        @pl.when(has_prev)
        def _():
            sent(down_copies(sec))

        @pl.when(sends_down)
        def _():
            sent(e_down_copies(sec))


def body(field, velocity, stiffness, curl_matrix, mass, connect, wall_index, dtn):
    n_mode = lax.axis_size("mode")
    n_mer = lax.axis_size("mer")
    mode_dev, _, nodes = field.shape
    modes = mode_dev * n_mode
    nphi = velocity.shape[1]
    elems, npe = connect.shape
    wall_dev = wall_index.shape[0]
    rows = mode_dev * PAD
    chunk = nodes // n_mode
    ghosts = GHOST // chunk
    forward, inverse = transforms(modes, nphi)
    sems = 4 * n_mode + n_mer + 3
    vmem = pl.BlockSpec(memory_space=pltpu.VMEM)
    return pl.pallas_call(
        functools.partial(kernel, n_mode, n_mer, modes),
        out_shape=(
            jax.ShapeDtypeStruct(field.shape, F32),
            jax.ShapeDtypeStruct((2, mode_dev, 2, wall_dev), F32),
        ),
        in_specs=[vmem] * 10,
        out_specs=(vmem, vmem),
        scratch_shapes=[
            pltpu.VMEM((2, rows, nodes), BF),
            pltpu.VMEM((2, n_mode, rows, chunk), BF),
            pltpu.VMEM((2, n_mode, rows, chunk), BF),
            pltpu.VMEM((2, rows, nodes), BF),
            pltpu.VMEM((2, rows, GHOST), BF),
            pltpu.VMEM((2, n_mode, rows, chunk), BF),
            pltpu.VMEM((2, n_mode, rows, chunk), BF),
            pltpu.VMEM((2, n_mode, rows, chunk), BF),
            pltpu.VMEM((2, ghosts, rows, chunk), BF),
            pltpu.VMEM((2, 2 * mode_dev, 128), BF),
            pltpu.VMEM((2, n_mer, 2 * mode_dev, 128), BF),
            pltpu.VMEM((elems, npe), jnp.int32),
            pltpu.VMEM((2, 256, 256), BF),
            pltpu.VMEM((nodes + GHOST, elems * npe), BF),
            pltpu.VMEM((2 * (nodes // 256) + 2, nodes + GHOST, 256), BF),
            pltpu.VMEM((nodes, 128), BF),
            pltpu.SemaphoreType.DMA((2, sems)),
            pltpu.SemaphoreType.DMA((2, sems)),
        ],
        compiler_params=pltpu.CompilerParams(
            collective_id=0, has_side_effects=True, vmem_limit_bytes=40 * 1024 * 1024
        ),
    )(
        field,
        velocity,
        stiffness,
        curl_matrix,
        mass.reshape(1, nodes),
        connect,
        wall_index.reshape(1, wall_dev),
        dtn,
        forward,
        inverse,
    )


def solution(mesh):
    placed = (
        P("mode", None, "mer"),
        P(None, None, ("mer", "mode")),
        P(),
        P(),
        P("mer"),
        P("mer", None),
        P("mer"),
        P("mode", "mer", None),
    )
    return jax.shard_map(
        body,
        mesh=mesh,
        in_specs=placed,
        out_specs=(P("mode", None, "mer"), P(None, "mode", None, "mer")),
        check_vma=False,
    )
```

time: 127 us -> 30 us (0.24)
  blocking collectives: 31.8 us -> 0 us
  starting transfers between devices: 29.9 us -> 0 us
  Pallas kernels: 0 us -> 22.3 us
  other arithmetic: 19.3 us -> 0 us
  waiting for transfers between devices: 13.9 us -> 0 us
  matrix products: 11.8 us -> 0 us
  local copies, waits for them, and re-layouts: 17.5 us -> 6.39 us
    all_gather x2 -> x0, blocking collectives: 31.8 us -> none  [rate(): whole = lax.all_gather(trace, 'mer', axis=2, tiled=True)]
    pallas_call x0 -> x1, Pallas kernels: none -> 22.3 us  [body(): pl.pallas_call(functools.partial(kernel, n_mode, n_mer, modes), out_shape...]
    all_to_all x4 -> x0, starting transfers between devices: 16.9 us -> none  [the longest x2 8.47 us: rate(): lax.all_to_all(field, 'mode', split_axis=2, concat_axis=0, tiled=True)]
    scatter-add x6 -> x0, other arithmetic: 14.9 us -> none  [the longest x2 7.43 us: rate(): total = total.at[:, 2, wall_index].add(-0.5 * flux[:, 0])]
    ppermute x6 -> x0, starting transfers between devices: 13 us -> none  [from_behind(): return lax.ppermute(block, axis, route)]
    dot_general x30 -> x0, matrix products: 11.8 us -> none  [the longest x4 2.04 us: step(): lax.dot_general(rows_hi, onehot, (((1,), (1,)), ((), ())), preferred_elem...]
    all_to_all x4 -> x0, waiting for transfers between devices: 9.75 us -> none  [the longest x2 9.74 us: rate(): emf = lax.all_to_all(back, 'mode', split_axis=0, concat_axis=2, tiled=True)]
    ppermute x6 -> x0, waiting for transfers between devices: 4.11 us -> none  [from_behind(): return lax.ppermute(block, axis, route)]
  transfers between devices with their start and end apart: 10 -> 0, of which waited for: 5 -> 0; matrix products, arithmetic and copies ran while one was open for 11% -> 0% of each run, Pallas kernels for 0% -> 0%
where the time goes in v1:
time: 30 us; the launch traced here: 29.4 us
  Pallas kernels  22.3 us (74%)
  local copies, waits for them, and re-layouts  6.39 us (21%)
  between operations  0.72 us (2%)
    pallas_call x1, Pallas kernels, body(): pl.pallas_call(functools.partial(kernel, n_mode, n_mer, modes), out_shape...  22.3 us
    unnamed x20, local copies, waits for them, and re-layouts  5.69 us
    pallas_call x1, local copies, waits for them, and re-layouts, body(): pl.pallas_call(functools.partial(kernel, n_mode, n_mer, modes), out_shape...  0.7 us

profile of v1, /device:TPU:0, one launch (start us, length us, event | category | flops | bytes accessed | tf_op | source)
XLA Modules:
  0.0 29.4 jit_solution(2328845708338753309)
XLA Ops:
  0.6 0.0 copy-start.1
  0.6 0.0 copy-start.2
  0.7 0.0 copy-start.7
  0.7 0.0 copy-start.8
  0.7 1.0 %copy.12.field_ref = f32[8,6,512]{2,1,0:T(8,128)S(1)} copy(f32[8,6,512]{2,0,1:T(8,128)} %param.10) | data formatting | bytes 196608 | tf_op args[0]
  1.7 0.0 copy-done.1
  1.7 0.0 copy-done.2
  1.7 0.0 copy-done.7
  1.7 0.0 copy-done.8
  1.7 0.0 copy-start
  1.7 1.0 %copy-done = bf16[8,64,512]{2,1,0:T(8,128)(2,1)S(1)} copy-done((bf16[8,64,512]{2,1,0:T(8,128)(2,1)S(1)}, bf16[8,64,512]{2,1,0:T(8,128)(2,1)}, u32[]{:S(2)}) %copy-start) | copy-done | bytes 524312
  2.8 0.0 copy-start.3
  2.8 0.8 %copy-done.3 = bf16[3,64,128]{2,1,0:T(8,128)(2,1)S(1)} copy-done((bf16[3,64,128]{2,1,0:T(8,128)(2,1)S(1)}, bf16[3,64,128]{2,1,0:T(8,128)(2,1)}, u32[]{:S(2)}) %copy-start.3) | copy-done | bytes 49176
  3.6 0.0 copy-start.4
  3.6 0.8 %copy-done.4 = f32[64,64]{1,0:T(8,128)S(1)} copy-done((f32[64,64]{1,0:T(8,128)S(1)}, f32[64,64]{1,0:T(8,128)}, u32[]{:S(2)}) %copy-start.4) | copy-done | bytes 16408
  4.3 0.0 copy-start.5
  4.3 0.8 %copy-done.5 = f32[64,64]{1,0:T(8,128)S(1)} copy-done((f32[64,64]{1,0:T(8,128)S(1)}, f32[64,64]{1,0:T(8,128)}, u32[]{:S(2)}) %copy-start.5) | copy-done | bytes 16408
  5.1 0.0 copy-start.6
  5.1 0.7 %copy-done.6 = s32[16,64]{1,0:T(8,128)S(1)} copy-done((s32[16,64]{1,0:T(8,128)S(1)}, s32[16,64]{1,0:T(8,128)}, u32[]{:S(2)}) %copy-start.6) | copy-done | bytes 4120
  5.8 22.3 %shard_map.113 = (f32[8,6,512]{2,1,0:T(8,128)S(1)}, f32[2,8,2,64]{3,2,1,0:T(2,128)S(1)}) custom-call(f32[8,6,512]{2,1,0:T(8,128)S(1)} %copy.12.field_ref, bf16[3,64,128]{2,1,0:T(8,128)(2,1)S(1)} %copy-done.3, f32[64,64]{1,0:T(8,128)S(1)} %copy-done.4, f32[64,64]{1,0:T(8,128)S(1)} %copy-done.5, f32[1,512]{1,0:T(1,128)S(1)} %bitcast.2, ...), custom_call_target="tpu_custom_call" | custom-call | tf_op jit(solution)/shard_map/pallas_call | solution.py:430
  28.1 0.7 %copy.13 = f32[8,6,512]{2,0,1:T(8,128)} copy(f32[8,6,512]{2,1,0:T(8,128)S(1)} %get-tuple-element.2) | data formatting | bytes 196608 | tf_op jit(solution)/shard_map/pallas_call | solution.py:430
  28.8 0.6 %copy.15 = f32[2,8,2,64]{3,2,1,0:T(2,128)} copy(f32[2,8,2,64]{3,2,1,0:T(2,128)S(1)} %get-tuple-element.7) | data formatting | bytes 16384
Async XLA Ops:
  0.6 1.1 %copy-start.1 = (bf16[256,192]{1,0:T(8,128)(2,1)S(1)}, bf16[256,192]{1,0:T(8,128)(2,1)}, u32[]{:S(2)}) copy-start(bf16[256,192]{1,0:T(8,128)(2,1)} %constant.5.clone.inverse_ref) | copy-start | bytes 294916
  0.6 1.1 %copy-start.2 = (bf16[192,256]{1,0:T(8,128)(2,1)S(1)}, bf16[192,256]{1,0:T(8,128)(2,1)}, u32[]{:S(2)}) copy-start(bf16[192,256]{1,0:T(8,128)(2,1)} %constant.4.clone.forward_ref) | copy-start | bytes 294916
  0.7 1.1 %copy-start.7 = (f32[512]{0:T(512)S(1)}, f32[512]{0:T(512)}, u32[]{:S(2)}) copy-start(f32[512]{0:T(512)} %param.14) | copy-start | bytes 6148
  0.7 1.1 %copy-start.8 = (s32[64]{0:T(128)S(1)}, s32[64]{0:T(128)}, u32[]{:S(2)}) copy-start(s32[64]{0:T(128)} %param.16) | copy-start | bytes 772
  1.7 1.0 %copy-start = (bf16[8,64,512]{2,1,0:T(8,128)(2,1)S(1)}, bf16[8,64,512]{2,1,0:T(8,128)(2,1)}, u32[]{:S(2)}) copy-start(bf16[8,64,512]{2,1,0:T(8,128)(2,1)} %dtn_ref.1) | copy-start | bytes 1572868
  2.8 0.8 %copy-start.3 = (bf16[3,64,128]{2,1,0:T(8,128)(2,1)S(1)}, bf16[3,64,128]{2,1,0:T(8,128)(2,1)}, u32[]{:S(2)}) copy-start(bf16[3,64,128]{2,1,0:T(8,128)(2,1)} %vel_ref.1) | copy-start | bytes 147460
  3.6 0.8 %copy-start.4 = (f32[64,64]{1,0:T(8,128)S(1)}, f32[64,64]{1,0:T(8,128)}, u32[]{:S(2)}) copy-start(f32[64,64]{1,0:T(8,128)} %stiff_ref.1) | copy-start | bytes 49156
  4.3 0.8 %copy-start.5 = (f32[64,64]{1,0:T(8,128)S(1)}, f32[64,64]{1,0:T(8,128)}, u32[]{:S(2)}) copy-start(f32[64,64]{1,0:T(8,128)} %curl_ref.1) | copy-start | bytes 49156
  5.1 0.7 %copy-start.6 = (s32[16,64]{1,0:T(8,128)S(1)}, s32[16,64]{1,0:T(8,128)}, u32[]{:S(2)}) copy-start(s32[16,64]{1,0:T(8,128)} %connect_ref.1) | copy-start | bytes 12292

commit v2 on v1

--- a/solution.py
+++ b/solution.py
@@ -9,24 +9,24 @@
 from jax.sharding import PartitionSpec as P
 
 GHOST = 256
-PAD = 8
 MESH = pl.DeviceIdType.MESH
 BF = jnp.bfloat16
 F32 = jnp.float32
 
 
-def transforms(modes, nphi):
+def transforms(modes, mode_dev, nphi):
     angle = 2.0 * np.pi * ((np.arange(modes)[:, None] * np.arange(nphi)[None, :]) % nphi) / nphi
     table = np.stack([np.cos(angle), -np.sin(angle)], 1)
-    forward = np.zeros((3, nphi, modes, PAD))
-    inverse = np.zeros((modes, PAD, 3, nphi))
+    forward = np.zeros((3, nphi, modes, 6))
+    inverse = np.zeros((modes, 6, 3, nphi))
     for p in range(2):
         for c in range(3):
             forward[c, :, :, 3 * p + c] = table[:, p].T
             inverse[:, 3 * p + c, (c - 1) % 3, :] = table[:, p] / nphi
-    forward = forward.reshape(3 * nphi, modes * PAD)
-    inverse = inverse.reshape(modes * PAD, 3 * nphi)
-    return jnp.asarray(forward, BF), jnp.asarray(inverse, BF)
+    owners = modes // mode_dev
+    forward = forward.reshape(3 * nphi, owners, mode_dev, 6).transpose(0, 1, 3, 2).reshape(3 * nphi, modes * 6)
+    inverse = inverse.reshape(owners, mode_dev, 6, 3 * nphi).transpose(0, 2, 1, 3).reshape(modes * 6, 3 * nphi)
+    return jnp.asarray(forward, F32), jnp.asarray(inverse, F32)
 
 
 def mm(a, b):
@@ -49,16 +49,16 @@
     n_mode,
     n_mer,
     modes,
-    field_ref,
-    vel_ref,
-    stiff_ref,
-    curl_ref,
-    mass_ref,
-    connect_ref,
-    wall_ref,
-    dtn_ref,
-    forward_ref,
-    inverse_ref,
+    field_in,
+    vel_in,
+    stiff_in,
+    curl_in,
+    mass_in,
+    connect_in,
+    wall_in,
+    dtn_in,
+    forward_in,
+    inverse_in,
     out_ref,
     flux_ref,
     f_full,
@@ -75,14 +75,24 @@
     c_prev,
     kmat,
     pick,
-    oper,
     wall_hot,
+    field_ref,
+    vel_ref,
+    stiff_ref,
+    curl_ref,
+    mass_ref,
+    connect_ref,
+    wall_ref,
+    dtn_ref,
+    forward_ref,
+    inverse_ref,
     send_sem,
     recv_sem,
+    load_sem,
 ):
-    mode_dev, _, nodes = field_ref.shape
+    _, mode_dev, nodes = field_ref.shape
     nphi = vel_ref.shape[1]
-    rows = mode_dev * PAD
+    rows = mode_dev * 6
     chunk = nodes // n_mode
     ghosts = GHOST // chunk
     elems, npe = connect_ref.shape
@@ -103,6 +113,26 @@
     def other_mer(k):
         return lax.rem(d + k, n_mer)
 
+    loads = [
+        pltpu.make_async_copy(src, dst, load_sem.at[i])
+        for i, (src, dst) in enumerate(
+            [
+                (field_in, field_ref),
+                (connect_in, connect_ref),
+                (wall_in, wall_ref),
+                (stiff_in, stiff_ref),
+                (curl_in, curl_ref),
+                (forward_in, forward_ref),
+                (vel_in, vel_ref),
+                (inverse_in, inverse_ref),
+                (dtn_in, dtn_ref),
+                (mass_in, mass_ref),
+            ]
+        )
+    ]
+    for load in loads:
+        load.start()
+
     barrier = pltpu.get_barrier_semaphore()
 
     def greet(mode, mer):
@@ -199,24 +229,7 @@
     def arrive(ref, sec, no):
         copy(ref, ref, sec, no, no, me, d).wait_recv()
 
-    field = jnp.concatenate(
-        [
-            part
-            for m in range(mode_dev)
-            for part in (field_ref[m], jnp.zeros((PAD - 6, nodes), F32))
-        ],
-        0,
-    )
     halves = 128 // wall_dev
-    wall_row = jnp.concatenate([wall_ref[...]] * halves, 1)
-    lane = iota((1, 128), 1)
-    wall_row = jnp.where(lane // wall_dev == lax.rem(d, halves), wall_row, -1)
-    wall_hot[...] = onehot(iota((nodes, 128), 0) == wall_row)
-
-    take_row = iota((2 * mode_dev, rows), 0)
-    take = onehot(iota((2 * mode_dev, rows), 1) == (take_row // 2) * PAD + 2 + 3 * (take_row % 2))
-    put_row = iota((rows, 2 * mode_dev), 1)
-    put = onehot(iota((rows, 2 * mode_dev), 0) == (put_row // 2) * PAD + 2 + 3 * (put_row % 2))
 
     def stage(sec, value):
         low = value.astype(BF)
@@ -226,7 +239,9 @@
         f_got[sec, me] = f_part[sec, me]
 
     def stage_trace(sec):
-        walls = mm(mm(take, f_full[sec]).astype(BF), wall_hot[...]).astype(BF)
+        low = f_full[sec]
+        picked = jnp.concatenate([low[r * mode_dev : (r + 1) * mode_dev] for r in (2, 5)], 0)
+        walls = mm(picked, wall_hot[...]).astype(BF)
         t_part[sec] = walls
         t_got[sec, d] = walls
 
@@ -241,6 +256,8 @@
         def _():
             start(down_copies(sec))
 
+    loads[0].wait()
+    field = field_ref[...].reshape(rows, nodes)
     stage(0, field)
 
     @pl.when(jnp.logical_not(has_prev))
@@ -258,59 +275,65 @@
     next_n = has_next.astype(jnp.int32)
     pl.semaphore_wait(barrier, n_mode - 1 + n_mer - 1 + (n_mode - 1) * (prev_n + next_n))
 
+    loads[1].wait()
     send_field(0)
+
+    step = 128
+
+    def fill_pick(which, ref):
+        numbers = jnp.concatenate([ref[e : e + 1, :] for e in range(elems)], 1)
+
+        def fill(i, carry):
+            base = pl.multiple_of(i * step, step)
+            pick[which, pl.ds(base, step), :] = onehot(iota((step, slots), 0) + base == numbers)
+            return carry
+
+        lax.fori_loop(0, ext // step, fill, 0)
+
+    loads[2].wait()
+    wall_row = jnp.concatenate([wall_ref[...]] * halves, 1)
+    lane = iota((1, 128), 1)
+    wall_row = jnp.where(lane // wall_dev == lax.rem(d, halves), wall_row, -1)
+    wall_hot[...] = onehot(iota((nodes, 128), 0) == wall_row)
     stage_trace(0)
     start(t_copies(0))
 
-    group = 256 // npe
-    same = iota((256, 256), 0) // npe == iota((256, 256), 1) // npe
+    fill_pick(0, connect_ref)
+
+    wide_dim = 256
+    group = wide_dim // npe
+    groups = slots // wide_dim
+    same = iota((wide_dim, wide_dim), 0) // npe == iota((wide_dim, wide_dim), 1) // npe
 
     def spread(ref, sign):
-        wide = jnp.concatenate([sign * ref[...]] * group, 1)
-        return jnp.where(same, jnp.concatenate([wide] * group, 0), 0.0).astype(BF)
-
+        turned = jnp.concatenate([sign * ref[...].T] * group, 1)
+        return jnp.where(same, jnp.concatenate([turned] * group, 0), 0.0).astype(BF)
+
+    loads[3].wait()
     kmat[0] = spread(stiff_ref, -1.0)
+    loads[4].wait()
     kmat[1] = spread(curl_ref, 1.0)
-    blocks = nodes // 256
-    step = 128
-
-    def fill_pick(ref):
-        numbers = jnp.concatenate([ref[e : e + 1, :] for e in range(elems)], 1)
-
-        def fill(i, carry):
-            base = pl.multiple_of(i * step, step)
-            pick[pl.ds(base, step), :] = onehot(iota((step, slots), 0) + base == numbers)
-            return carry
-
-        lax.fori_loop(0, ext // step, fill, 0)
-
-    def build(index, first, which):
-        take_rows = pick[pl.ds(pl.multiple_of(first, 256), 256), :]
-        moved = jnp.concatenate(
-            [mm(take_rows[:, g * 256 : (g + 1) * 256], kmat[which]).astype(BF) for g in range(slots // 256)], 1
+
+    for load in loads[5:]:
+        load.wait()
+    mass_inv = 1.0 / mass_ref[...]
+    mode_no = me * mode_dev + lax.rem(iota((rows, 1), 0), mode_dev)
+    damp = 4.0 * (mode_no.astype(F32) / modes) ** 2
+
+    def local(own, nxt, prv, which):
+        here = mm(jnp.concatenate([own, nxt], 1), pick[0]).astype(BF)
+        back = mm(jnp.concatenate([prv, own[:, :GHOST]], 1), pick[1]).astype(BF)
+        tall = jnp.concatenate(
+            [x[:, g * wide_dim : (g + 1) * wide_dim] for x in (here, back) for g in range(groups)], 0
         )
-        oper[index] = mm_t(pick[...], moved).astype(BF)
-
-    def build_own(i, carry):
-        build(i, lax.rem(i, blocks) * 256, i // blocks)
-        return carry
-
-    def build_prev(i, carry):
-        build(2 * blocks + i, nodes, i)
-        return carry
-
-    fill_pick(connect_ref)
-    lax.fori_loop(0, 2 * blocks, build_own, 0)
-
-    mass_inv = 1.0 / mass_ref[...]
-    mode_no = me * mode_dev + iota((rows, 1), 0) // PAD
-    damp = 4.0 * (mode_no.astype(F32) / modes) ** 2
-
-    def apply(own, nxt, prv, which):
-        here = jnp.concatenate([own, nxt], 1)
-        sums = [mm(here, oper[which * blocks + b]) for b in range(blocks)]
-        sums[0] = sums[0] + mm(jnp.concatenate([prv, own[:, :GHOST]], 1), oper[2 * blocks + which])
-        return jnp.concatenate(sums, 1)
+        done = mm(tall, kmat[which])
+        return [done[i * rows : (i + 1) * rows] for i in range(2 * groups)]
+
+    def scatter(parts):
+        low = [x.astype(BF) for x in parts]
+        total = mm_t(jnp.concatenate(low[:groups], 1), pick[0, :nodes, :])
+        extra = mm_t(jnp.concatenate(low[groups:], 1), pick[1, nodes:, :])
+        return jnp.concatenate([total[:, :GHOST] + extra, total[:, GHOST:]], 1)
 
     def lanes(ref, sec, count):
         return jnp.concatenate([ref[sec, j] for j in range(count)], 1)
@@ -318,11 +341,11 @@
     def rate(sec, value):
         for k in range(1, n_mode):
             arrive(f_got.at[sec, other_mode(k)], sec, s_f + other_mode(k))
-        phys = mm(forward_ref[...], f_got[sec].reshape(n_mode * rows, chunk))
+        phys = mm(forward_ref[...].astype(BF), f_got[sec].reshape(n_mode * rows, chunk))
         px, py, pz = [phys[c * nphi : (c + 1) * nphi] for c in range(3)]
         vx, vy, vz = [vel_ref[c].astype(F32) for c in range(3)]
         cross = jnp.concatenate([vy * pz - vz * py, vz * px - vx * pz, vx * py - vy * px], 0)
-        emf = mm(inverse_ref[...], cross.astype(BF)).astype(BF)
+        emf = mm(inverse_ref[...].astype(BF), cross.astype(BF)).astype(BF)
         e_part[sec] = emf.reshape(n_mode, rows, chunk)
         e_own[sec, me] = e_part[sec, me]
         start(e_copies(sec))
@@ -341,8 +364,7 @@
             def _():
                 arrive(c_prev, sec, s_c)
 
-            fill_pick(c_prev)
-            lax.fori_loop(0, 2, build_prev, 0)
+            fill_pick(1, c_prev)
 
         @pl.when(has_prev)
         def _():
@@ -352,7 +374,7 @@
         def _():
             arrive(f_next.at[sec], sec, s_fn)
 
-        total = apply(f_full[sec], f_next[sec], f_prev[sec], 0)
+        diffused = local(f_full[sec], f_next[sec], f_prev[sec], 0)
 
         for k in range(1, n_mer):
             arrive(t_got.at[sec, other_mer(k)], sec, s_t + other_mer(k))
@@ -360,13 +382,14 @@
             [sum([t_got[sec, i + h] for h in range(1, halves)], t_got[sec, i]) for i in range(0, n_mer, halves)], 1
         )
         wide = mm_t(trace, dtn_ref[...].reshape(mode_dev * wall_dev, trace.shape[1]))
-        wide = jnp.where(iota(wide.shape, 1) // wall_dev == iota(wide.shape, 0) // 2, wide, 0.0)
+        wide = jnp.where(iota(wide.shape, 1) // wall_dev == lax.rem(iota(wide.shape, 0), mode_dev), wide, 0.0)
         folded = sum([wide[:, i : i + 128] for i in range(128, wide.shape[1], 128)], wide[:, :128])
         flux = sum([folded[:, h * wall_dev : (h + 1) * wall_dev] for h in range(1, halves)], folded[:, :wall_dev])
         for m in range(mode_dev):
-            flux_ref[sec, m] = flux[2 * m : 2 * m + 2]
+            flux_ref[sec, m] = jnp.concatenate([flux[m : m + 1], flux[mode_dev + m : mode_dev + m + 1]], 0)
         spots = mm_t(jnp.concatenate([-0.5 * flux] * halves, 1).astype(BF), wall_hot[...])
-        total = total + mm(put, spots.astype(BF))
+        blank = jnp.zeros((2 * mode_dev, nodes), F32)
+        pulled = jnp.concatenate([blank, spots[:mode_dev], blank, spots[mode_dev:]], 0)
 
         for k in range(1, n_mode):
             arrive(e_own.at[sec, other_mode(k)], sec, s_eo + other_mode(k))
@@ -381,7 +404,8 @@
             for j in range(ghosts):
                 arrive(e_next.at[sec, j], sec, s_en + j)
 
-        total = total + apply(lanes(e_own, sec, n_mode), lanes(e_next, sec, ghosts), lanes(e_prev, sec, n_mode), 1)
+        curled = local(lanes(e_own, sec, n_mode), lanes(e_next, sec, ghosts), lanes(e_prev, sec, n_mode), 1)
+        total = scatter([x + y for x, y in zip(diffused, curled)]) + pulled
         return total * mass_inv - damp * value
 
     section = field + 0.2 * rate(0, field)
@@ -391,8 +415,7 @@
     start(t_copies(1))
     second = rate(1, section)
     advanced = 0.5 * (field + section + 0.2 * second)
-    for m in range(mode_dev):
-        out_ref[m] = advanced[m * PAD : m * PAD + 6]
+    out_ref[...] = advanced.reshape(out_ref.shape)
 
     for sec in range(2):
         sent(f_copies(sec))
@@ -421,19 +444,20 @@
     nphi = velocity.shape[1]
     elems, npe = connect.shape
     wall_dev = wall_index.shape[0]
-    rows = mode_dev * PAD
+    rows = mode_dev * 6
     chunk = nodes // n_mode
     ghosts = GHOST // chunk
-    forward, inverse = transforms(modes, nphi)
+    forward, inverse = transforms(modes, mode_dev, nphi)
     sems = 4 * n_mode + n_mer + 3
     vmem = pl.BlockSpec(memory_space=pltpu.VMEM)
-    return pl.pallas_call(
+    hbm = pl.BlockSpec(memory_space=pltpu.HBM)
+    advanced, flux = pl.pallas_call(
         functools.partial(kernel, n_mode, n_mer, modes),
         out_shape=(
-            jax.ShapeDtypeStruct(field.shape, F32),
+            jax.ShapeDtypeStruct((6, mode_dev, nodes), F32),
             jax.ShapeDtypeStruct((2, mode_dev, 2, wall_dev), F32),
         ),
-        in_specs=[vmem] * 10,
+        in_specs=[hbm] * 10,
         out_specs=(vmem, vmem),
         scratch_shapes=[
             pltpu.VMEM((2, rows, nodes), BF),
@@ -449,17 +473,27 @@
             pltpu.VMEM((2, n_mer, 2 * mode_dev, 128), BF),
             pltpu.VMEM((elems, npe), jnp.int32),
             pltpu.VMEM((2, 256, 256), BF),
-            pltpu.VMEM((nodes + GHOST, elems * npe), BF),
-            pltpu.VMEM((2 * (nodes // 256) + 2, nodes + GHOST, 256), BF),
+            pltpu.VMEM((2, nodes + GHOST, elems * npe), BF),
             pltpu.VMEM((nodes, 128), BF),
+            pltpu.VMEM((6, mode_dev, nodes), F32),
+            pltpu.VMEM(velocity.shape, BF),
+            pltpu.VMEM(stiffness.shape, F32),
+            pltpu.VMEM(curl_matrix.shape, F32),
+            pltpu.VMEM((1, nodes), F32),
+            pltpu.VMEM(connect.shape, jnp.int32),
+            pltpu.VMEM((1, wall_dev), jnp.int32),
+            pltpu.VMEM(dtn.shape, BF),
+            pltpu.VMEM(forward.shape, F32),
+            pltpu.VMEM(inverse.shape, F32),
             pltpu.SemaphoreType.DMA((2, sems)),
             pltpu.SemaphoreType.DMA((2, sems)),
+            pltpu.SemaphoreType.DMA((10,)),
         ],
         compiler_params=pltpu.CompilerParams(
-            collective_id=0, has_side_effects=True, vmem_limit_bytes=40 * 1024 * 1024
+            collective_id=0, has_side_effects=True, vmem_limit_bytes=60 * 1024 * 1024
         ),
     )(
-        field,
+        jnp.swapaxes(field, 0, 1),
         velocity,
         stiffness,
         curl_matrix,
@@ -470,6 +504,7 @@
         forward,
         inverse,
     )
+    return jnp.swapaxes(advanced, 0, 1), flux
 
 
 def solution(mesh):

time: 30 us -> 26.6 us (0.89); the launches traced: 29.4 us -> 26.3 us
  local copies, waits for them, and re-layouts: 6.39 us -> 2.15 us
  Pallas kernels: 22.3 us -> 23.5 us
    unnamed x20 -> x4, local copies, waits for them, and re-layouts: 5.69 us -> 2.15 us
    pallas_call x1, Pallas kernels: 22.3 us -> 23.5 us  [body(): pl.pallas_call(functools.partial(kernel, n_mode, n_mer, modes), out_shape...]
    pallas_call x1 -> x0, local copies, waits for them, and re-layouts: 0.7 us -> none  [body(): pl.pallas_call(functools.partial(kernel, n_mode, n_mer, modes), out_shape...]
where the time goes in v2:
time: 26.6 us; the launch traced here: 26.3 us
  Pallas kernels  23.5 us (88%)
  local copies, waits for them, and re-layouts  2.15 us (8%)
  between operations  0.65 us (2%)
    pallas_call x1, Pallas kernels, body(): pl.pallas_call(functools.partial(kernel, n_mode, n_mer, modes), out_shape...  23.5 us
    unnamed x4, local copies, waits for them, and re-layouts  2.15 us

profile of v2, /device:TPU:0, one launch (start us, length us, event | category | flops | bytes accessed | tf_op | source)
XLA Modules:
  0.0 26.3 jit_solution(15221633402238740998)
XLA Ops:
  0.6 23.5 %shard_map.113 = (f32[6,8,512]{2,1,0:T(8,128)}, f32[2,8,2,64]{3,2,1,0:T(2,128)}) custom-call(f32[6,8,512]{2,1,0:T(8,128)} %bitcast.4, bf16[3,64,128]{2,1,0:T(8,128)(2,1)} %vel_in.1, f32[64,64]{1,0:T(8,128)} %stiff_in.1, f32[64,64]{1,0:T(8,128)} %curl_in.1, f32[1,512]{1,0:T(1,128)} %bitcast.6, s32[16,64]{1,0:T(8,128)} %connect_in.1, s32[1,64]{1,0:T(1,128)} %bitcast.7, ...), custom_call_target="tpu_custom_call" | custom-call | tf_op jit(solution)/shard_map/pallas_call | solution.py:454
  24.2 0.0 copy-start
  24.2 1.5 %copy.14 = f32[8,6,512]{2,0,1:T(8,128)} copy(f32[8,6,512]{2,0,1:T(8,128)} %bitcast.5) | data formatting | bytes 196608
  25.7 0.0 copy-done
  25.7 0.6 %copy.15 = f32[2,8,2,64]{3,2,1,0:T(2,128)} copy(f32[2,8,2,64]{3,2,1,0:T(2,128)S(1)} %copy-done) | data formatting | bytes 16384
Async XLA Ops:
  24.2 1.6 %copy-start = (f32[2,8,2,64]{3,2,1,0:T(2,128)S(1)}, f32[2,8,2,64]{3,2,1,0:T(2,128)}, u32[]{:S(2)}) copy-start(f32[2,8,2,64]{3,2,1,0:T(2,128)} %get-tuple-element.9) | copy-start | bytes 24580

commit v3 on v2

--- a/solution.py
+++ b/solution.py
@@ -130,8 +130,7 @@
             ]
         )
     ]
-    for load in loads:
-        load.start()
+    loads[0].start()
 
     barrier = pltpu.get_barrier_semaphore()
 
@@ -157,6 +156,9 @@
         @pl.when(jnp.logical_and(peer != d - 1, peer != d + 1))
         def _():
             greet(me, peer)
+
+    for load in loads[1:]:
+        load.start()
 
     s_f = 0
     s_eo = s_f + n_mode
@@ -298,8 +300,6 @@
     stage_trace(0)
     start(t_copies(0))
 
-    fill_pick(0, connect_ref)
-
     wide_dim = 256
     group = wide_dim // npe
     groups = slots // wide_dim
@@ -309,10 +309,18 @@
         turned = jnp.concatenate([sign * ref[...].T] * group, 1)
         return jnp.where(same, jnp.concatenate([turned] * group, 0), 0.0).astype(BF)
 
-    loads[3].wait()
-    kmat[0] = spread(stiff_ref, -1.0)
-    loads[4].wait()
-    kmat[1] = spread(curl_ref, 1.0)
+    def prepare():
+        fill_pick(0, connect_ref)
+        loads[3].wait()
+        kmat[0] = spread(stiff_ref, -1.0)
+        loads[4].wait()
+        kmat[1] = spread(curl_ref, 1.0)
+
+        @pl.when(has_prev)
+        def _():
+            arrive(c_prev, 0, s_c)
+
+        fill_pick(1, c_prev)
 
     for load in loads[5:]:
         load.wait()
@@ -320,14 +328,20 @@
     mode_no = me * mode_dev + lax.rem(iota((rows, 1), 0), mode_dev)
     damp = 4.0 * (mode_no.astype(F32) / modes) ** 2
 
-    def local(own, nxt, prv, which):
-        here = mm(jnp.concatenate([own, nxt], 1), pick[0]).astype(BF)
-        back = mm(jnp.concatenate([prv, own[:, :GHOST]], 1), pick[1]).astype(BF)
-        tall = jnp.concatenate(
-            [x[:, g * wide_dim : (g + 1) * wide_dim] for x in (here, back) for g in range(groups)], 0
-        )
+    def elements(here, back, which):
+        low = (here.astype(BF), back.astype(BF))
+        tall = jnp.concatenate([x[:, g * wide_dim : (g + 1) * wide_dim] for x in low for g in range(groups)], 0)
         done = mm(tall, kmat[which])
         return [done[i * rows : (i + 1) * rows] for i in range(2 * groups)]
+
+    def gather_own(own):
+        return mm(own, pick[0, :nodes, :]), mm(own[:, :GHOST], pick[1, nodes:, :])
+
+    def gather_next(nxt):
+        return mm(nxt, pick[0, nodes:, :])
+
+    def gather_prev(prv):
+        return mm(prv, pick[1, :nodes, :])
 
     def scatter(parts):
         low = [x.astype(BF) for x in parts]
@@ -337,6 +351,24 @@
 
     def lanes(ref, sec, count):
         return jnp.concatenate([ref[sec, j] for j in range(count)], 1)
+
+    def all_sent(sec):
+        sent(f_copies(sec))
+        sent(t_copies(sec))
+        sent(e_copies(sec))
+
+        @pl.when(has_next)
+        def _():
+            sent(up_copies(sec))
+            sent(e_up_copies(sec))
+
+        @pl.when(has_prev)
+        def _():
+            sent(down_copies(sec))
+
+        @pl.when(sends_down)
+        def _():
+            sent(e_down_copies(sec))
 
     def rate(sec, value):
         for k in range(1, n_mode):
@@ -359,12 +391,9 @@
             start(e_down_copies(sec))
 
         if sec == 0:
-
-            @pl.when(has_prev)
-            def _():
-                arrive(c_prev, sec, s_c)
-
-            fill_pick(1, c_prev)
+            prepare()
+        else:
+            all_sent(0)
 
         @pl.when(has_prev)
         def _():
@@ -374,7 +403,8 @@
         def _():
             arrive(f_next.at[sec], sec, s_fn)
 
-        diffused = local(f_full[sec], f_next[sec], f_prev[sec], 0)
+        here, back = gather_own(f_full[sec])
+        diffused = elements(here + gather_next(f_next[sec]), back + gather_prev(f_prev[sec]), 0)
 
         for k in range(1, n_mer):
             arrive(t_got.at[sec, other_mer(k)], sec, s_t + other_mer(k))
@@ -393,18 +423,22 @@
 
         for k in range(1, n_mode):
             arrive(e_own.at[sec, other_mode(k)], sec, s_eo + other_mode(k))
+        here, back = gather_own(lanes(e_own, sec, n_mode))
 
         @pl.when(has_prev)
         def _():
             for j in range(n_mode):
                 arrive(e_prev.at[sec, j], sec, s_ep + j)
 
+        back = back + gather_prev(lanes(e_prev, sec, n_mode))
+
         @pl.when(has_next)
         def _():
             for j in range(ghosts):
                 arrive(e_next.at[sec, j], sec, s_en + j)
 
-        curled = local(lanes(e_own, sec, n_mode), lanes(e_next, sec, ghosts), lanes(e_prev, sec, n_mode), 1)
+        here = here + gather_next(lanes(e_next, sec, ghosts))
+        curled = elements(here, back, 1)
         total = scatter([x + y for x, y in zip(diffused, curled)]) + pulled
         return total * mass_inv - damp * value
 
@@ -417,23 +451,18 @@
     advanced = 0.5 * (field + section + 0.2 * second)
     out_ref[...] = advanced.reshape(out_ref.shape)
 
-    for sec in range(2):
-        sent(f_copies(sec))
-        sent(t_copies(sec))
-        sent(e_copies(sec))
-
-        @pl.when(has_next)
-        def _():
-            sent(up_copies(sec))
-            sent(e_up_copies(sec))
-
-        @pl.when(has_prev)
-        def _():
-            sent(down_copies(sec))
-
-        @pl.when(sends_down)
-        def _():
-            sent(e_down_copies(sec))
+    all_sent(1)
+
+
+def finish(out_in, flux_in, out_ref, flux_ref, sem):
+    copies = [
+        pltpu.make_async_copy(out_in, out_ref, sem.at[0]),
+        pltpu.make_async_copy(flux_in, flux_ref, sem.at[1]),
+    ]
+    for c in copies:
+        c.start()
+    for c in copies:
+        c.wait()
 
 
 def body(field, velocity, stiffness, curl_matrix, mass, connect, wall_index, dtn):
@@ -451,12 +480,13 @@
     sems = 4 * n_mode + n_mer + 3
     vmem = pl.BlockSpec(memory_space=pltpu.VMEM)
     hbm = pl.BlockSpec(memory_space=pltpu.HBM)
+    shapes = (
+        jax.ShapeDtypeStruct((6, mode_dev, nodes), F32),
+        jax.ShapeDtypeStruct((2, mode_dev, 2, wall_dev), F32),
+    )
     advanced, flux = pl.pallas_call(
         functools.partial(kernel, n_mode, n_mer, modes),
-        out_shape=(
-            jax.ShapeDtypeStruct((6, mode_dev, nodes), F32),
-            jax.ShapeDtypeStruct((2, mode_dev, 2, wall_dev), F32),
-        ),
+        out_shape=shapes,
         in_specs=[hbm] * 10,
         out_specs=(vmem, vmem),
         scratch_shapes=[
@@ -504,6 +534,14 @@
         forward,
         inverse,
     )
+    advanced, flux = pl.pallas_call(
+        finish,
+        out_shape=shapes,
+        in_specs=[hbm] * 2,
+        out_specs=(hbm, hbm),
+        scratch_shapes=[pltpu.SemaphoreType.DMA((2,))],
+        compiler_params=pltpu.CompilerParams(vmem_limit_bytes=60 * 1024 * 1024),
+    )(advanced, flux)
     return jnp.swapaxes(advanced, 0, 1), flux
 
 

time: 26.6 us -> 29.3 us (1.10)
  Pallas kernels: 23.5 us -> 28.5 us
  local copies, waits for them, and re-layouts: 2.15 us -> 0 us
    pallas_call x0 -> x1, Pallas kernels: none -> 4.59 us  [body(): pl.pallas_call(finish, out_shape=shapes, in_specs=[hbm] * 2, out_specs=(h...]
    unnamed x4 -> x0, local copies, waits for them, and re-layouts: 2.15 us -> none
    pallas_call x1, Pallas kernels: 23.5 us -> 23.9 us  [body(): pl.pallas_call(functools.partial(kernel, n_mode, n_mer, modes), out_shape...]
where the time goes in v3:
time: 29.3 us; the launch traced here: 29.1 us
  Pallas kernels  28.5 us (97%)
  between operations  0.64 us (2%)
    pallas_call x1, Pallas kernels, body(): pl.pallas_call(functools.partial(kernel, n_mode, n_mer, modes), out_shape...  23.9 us
    pallas_call x1, Pallas kernels, body(): pl.pallas_call(finish, out_shape=shapes, in_specs=[hbm] * 2, out_specs=(h...  4.59 us

profile of v3, /device:TPU:0, one launch (start us, length us, event | category | flops | bytes accessed | tf_op | source)
XLA Modules:
  0.0 29.1 jit_solution(8662014503856727982)
XLA Ops:
  0.6 23.9 %shard_map.113 = (f32[6,8,512]{2,1,0:T(8,128)}, f32[2,8,2,64]{3,2,1,0:T(2,128)}) custom-call(f32[6,8,512]{2,1,0:T(8,128)} %bitcast.4, bf16[3,64,128]{2,1,0:T(8,128)(2,1)} %vel_in.1, f32[64,64]{1,0:T(8,128)} %stiff_in.1, f32[64,64]{1,0:T(8,128)} %curl_in.1, f32[1,512]{1,0:T(1,128)} %bitcast.5, s32[16,64]{1,0:T(8,128)} %connect_in.1, s32[1,64]{1,0:T(1,128)} %bitcast.6, ...), custom_call_target="tpu_custom_call" | custom-call | tf_op jit(solution)/shard_map/pallas_call | solution.py:487
  24.5 4.6 %shard_map.114 = (f32[6,8,512]{2,1,0:T(8,128)}, f32[2,8,2,64]{3,2,1,0:T(2,128)}) custom-call(f32[6,8,512]{2,1,0:T(8,128)} %get-tuple-element.6.out_in, f32[2,8,2,64]{3,2,1,0:T(2,128)} %get-tuple-element.7.flux_in), custom_call_target="tpu_custom_call" | custom-call | tf_op jit(solution)/shard_map/pallas_call | solution.py:537

commit v4 on v3

--- a/solution.py
+++ b/solution.py
@@ -192,10 +192,10 @@
         ]
 
     def up_copies(sec):
-        made = [copy(f_full.at[sec], f_prev.at[sec], sec, s_fp, s_fp, me, d + 1)]
-        if sec == 0:
-            made.append(copy(connect_ref, c_prev, sec, s_c, s_c, me, d + 1))
-        return made
+        return [copy(f_full.at[sec], f_prev.at[sec], sec, s_fp, s_fp, me, d + 1)]
+
+    def connect_copies():
+        return [copy(connect_ref, c_prev, 0, s_c, s_c, me, d + 1)]
 
     def down_copies(sec):
         return [copy(f_full.at[sec, :, pl.ds(0, GHOST)], f_next.at[sec], sec, s_fn, s_fn, me, d - 1)]
@@ -258,10 +258,6 @@
         def _():
             start(down_copies(sec))
 
-    loads[0].wait()
-    field = field_ref[...].reshape(rows, nodes)
-    stage(0, field)
-
     @pl.when(jnp.logical_not(has_prev))
     def _():
         f_prev[...] = jnp.zeros(f_prev.shape, BF)
@@ -277,8 +273,12 @@
     next_n = has_next.astype(jnp.int32)
     pl.semaphore_wait(barrier, n_mode - 1 + n_mer - 1 + (n_mode - 1) * (prev_n + next_n))
 
+    loads[0].wait()
     loads[1].wait()
-    send_field(0)
+
+    @pl.when(has_next)
+    def _():
+        start(connect_copies())
 
     step = 128
 
@@ -297,9 +297,6 @@
     lane = iota((1, 128), 1)
     wall_row = jnp.where(lane // wall_dev == lax.rem(d, halves), wall_row, -1)
     wall_hot[...] = onehot(iota((nodes, 128), 0) == wall_row)
-    stage_trace(0)
-    start(t_copies(0))
-
     wide_dim = 256
     group = wide_dim // npe
     groups = slots // wide_dim
@@ -320,6 +317,10 @@
         def _():
             arrive(c_prev, 0, s_c)
 
+        @pl.when(has_next)
+        def _():
+            sent(connect_copies())
+
         fill_pick(1, c_prev)
 
     for load in loads[5:]:
@@ -352,19 +353,24 @@
     def lanes(ref, sec, count):
         return jnp.concatenate([ref[sec, j] for j in range(count)], 1)
 
-    def all_sent(sec):
+    def field_sent(sec):
         sent(f_copies(sec))
         sent(t_copies(sec))
+
+        @pl.when(has_next)
+        def _():
+            sent(up_copies(sec))
+
+        @pl.when(has_prev)
+        def _():
+            sent(down_copies(sec))
+
+    def emf_sent(sec):
         sent(e_copies(sec))
 
         @pl.when(has_next)
         def _():
-            sent(up_copies(sec))
             sent(e_up_copies(sec))
-
-        @pl.when(has_prev)
-        def _():
-            sent(down_copies(sec))
 
         @pl.when(sends_down)
         def _():
@@ -390,10 +396,9 @@
         def _():
             start(e_down_copies(sec))
 
-        if sec == 0:
+        @pl.when(sec == 0)
+        def _():
             prepare()
-        else:
-            all_sent(0)
 
         @pl.when(has_prev)
         def _():
@@ -421,6 +426,7 @@
         blank = jnp.zeros((2 * mode_dev, nodes), F32)
         pulled = jnp.concatenate([blank, spots[:mode_dev], blank, spots[mode_dev:]], 0)
 
+        field_sent(sec)
         for k in range(1, n_mode):
             arrive(e_own.at[sec, other_mode(k)], sec, s_eo + other_mode(k))
         here, back = gather_own(lanes(e_own, sec, n_mode))
@@ -439,30 +445,22 @@
 
         here = here + gather_next(lanes(e_next, sec, ghosts))
         curled = elements(here, back, 1)
+        emf_sent(sec)
         total = scatter([x + y for x, y in zip(diffused, curled)]) + pulled
         return total * mass_inv - damp * value
 
-    section = field + 0.2 * rate(0, field)
-    stage(1, section)
-    send_field(1)
-    stage_trace(1)
-    start(t_copies(1))
-    second = rate(1, section)
-    advanced = 0.5 * (field + section + 0.2 * second)
-    out_ref[...] = advanced.reshape(out_ref.shape)
-
-    all_sent(1)
-
-
-def finish(out_in, flux_in, out_ref, flux_ref, sem):
-    copies = [
-        pltpu.make_async_copy(out_in, out_ref, sem.at[0]),
-        pltpu.make_async_copy(flux_in, flux_ref, sem.at[1]),
-    ]
-    for c in copies:
-        c.start()
-    for c in copies:
-        c.wait()
+    out_ref[...] = field_ref[...]
+
+    def section(sec, carry):
+        value = out_ref[...].reshape(rows, nodes)
+        stage(sec, value)
+        send_field(sec)
+        stage_trace(sec)
+        start(t_copies(sec))
+        out_ref[...] = (value + 0.2 * rate(sec, value)).reshape(out_ref.shape)
+        return carry
+
+    lax.fori_loop(0, 2, section, 0)
 
 
 def body(field, velocity, stiffness, curl_matrix, mass, connect, wall_index, dtn):
@@ -484,7 +482,8 @@
         jax.ShapeDtypeStruct((6, mode_dev, nodes), F32),
         jax.ShapeDtypeStruct((2, mode_dev, 2, wall_dev), F32),
     )
-    advanced, flux = pl.pallas_call(
+    turned = jnp.swapaxes(field, 0, 1)
+    last, flux = pl.pallas_call(
         functools.partial(kernel, n_mode, n_mer, modes),
         out_shape=shapes,
         in_specs=[hbm] * 10,
@@ -523,7 +522,7 @@
             collective_id=0, has_side_effects=True, vmem_limit_bytes=60 * 1024 * 1024
         ),
     )(
-        jnp.swapaxes(field, 0, 1),
+        turned,
         velocity,
         stiffness,
         curl_matrix,
@@ -534,14 +533,7 @@
         forward,
         inverse,
     )
-    advanced, flux = pl.pallas_call(
-        finish,
-        out_shape=shapes,
-        in_specs=[hbm] * 2,
-        out_specs=(hbm, hbm),
-        scratch_shapes=[pltpu.SemaphoreType.DMA((2,))],
-        compiler_params=pltpu.CompilerParams(vmem_limit_bytes=60 * 1024 * 1024),
-    )(advanced, flux)
+    advanced = 0.5 * (turned + last)
     return jnp.swapaxes(advanced, 0, 1), flux
 
 

time: 29.3 us -> 27.5 us (0.939)
  Pallas kernels: 28.5 us -> 24.5 us
  other arithmetic: 0 us -> 1.55 us
  local copies, waits for them, and re-layouts: 0 us -> 0.61 us
    pallas_call x1 -> x0, Pallas kernels: 4.59 us -> none  [body(): pl.pallas_call(finish, out_shape=shapes, in_specs=[hbm] * 2, out_specs=(h...]
    transpose x0 -> x1, other arithmetic: none -> 1.55 us  [body(): return (jnp.swapaxes(advanced, 0, 1), flux)]
    pallas_call x1, Pallas kernels: 23.9 us -> 24.5 us  [body(): pl.pallas_call(functools.partial(kernel, n_mode, n_mer, modes), out_shape...]
    unnamed x0 -> x5, local copies, waits for them, and re-layouts: none -> 0.61 us
where the time goes in v4:
time: 27.5 us; the launch traced here: 27.3 us
  Pallas kernels  24.5 us (89%)
  other arithmetic  1.55 us (6%)
  between operations  0.67 us (2%)
  local copies, waits for them, and re-layouts  0.61 us (2%)
    pallas_call x1, Pallas kernels, body(): pl.pallas_call(functools.partial(kernel, n_mode, n_mer, modes), out_shape...  24.5 us
    transpose x1, other arithmetic, body(): return (jnp.swapaxes(advanced, 0, 1), flux)  1.55 us
    unnamed x5, local copies, waits for them, and re-layouts  0.61 us

profile of v4, /device:TPU:0, one launch (start us, length us, event | category | flops | bytes accessed | tf_op | source)
XLA Modules:
  0.0 27.3 jit_solution(9264967031381020450)
XLA Ops:
  0.6 0.0 copy-start
  0.6 24.5 %shard_map.113 = (f32[6,8,512]{2,1,0:T(8,128)}, f32[2,8,2,64]{3,2,1,0:T(2,128)}) custom-call(f32[6,8,512]{2,1,0:T(8,128)} %bitcast.6, bf16[3,64,128]{2,1,0:T(8,128)(2,1)} %vel_in.1, f32[64,64]{1,0:T(8,128)} %stiff_in.1, f32[64,64]{1,0:T(8,128)} %curl_in.1, f32[1,512]{1,0:T(1,128)} %bitcast.7, s32[16,64]{1,0:T(8,128)} %connect_in.1, s32[1,64]{1,0:T(1,128)} %bitcast.8, ...), custom_call_target="tpu_custom_call" | custom-call | tf_op jit(solution)/shard_map/pallas_call | solution.py:486
  25.1 0.0 copy-done
  25.2 0.0 copy-start.1
  25.2 1.6 %multiply_bitcast_fusion = f32[8,6,512]{2,0,1:T(8,128)} fusion(f32[6,8,512]{2,1,0:T(8,128)} %get-tuple-element.4, f32[8,6,512]{2,0,1:T(8,128)S(1)} %copy-done), kind=kLoop, calls=%fused_computation | loop fusion | flops 49152 | bytes 294912 | tf_op jit(solution)/shard_map/transpose | solution.py:537
  26.7 0.0 copy-done.1
  26.7 0.6 %copy.13 = f32[2,8,2,64]{3,2,1,0:T(2,128)} copy(f32[2,8,2,64]{3,2,1,0:T(2,128)S(1)} %copy-done.1) | data formatting | bytes 16384
Async XLA Ops:
  0.6 24.5 %copy-start = (f32[8,6,512]{2,0,1:T(8,128)S(1)}, f32[8,6,512]{2,0,1:T(8,128)}, u32[]{:S(2)}) copy-start(f32[8,6,512]{2,0,1:T(8,128)} %param.10) | copy-start | bytes 294916
  25.2 1.6 %copy-start.1 = (f32[2,8,2,64]{3,2,1,0:T(2,128)S(1)}, f32[2,8,2,64]{3,2,1,0:T(2,128)}, u32[]{:S(2)}) copy-start(f32[2,8,2,64]{3,2,1,0:T(2,128)} %get-tuple-element.9) | copy-start | bytes 24580

commit v5 on v3

--- a/solution.py
+++ b/solution.py
@@ -160,61 +160,54 @@
     for load in loads[1:]:
         load.start()
 
-    s_f = 0
-    s_eo = s_f + n_mode
-    s_ep = s_eo + n_mode
-    s_en = s_ep + n_mode
-    s_fp = s_en + n_mode
-    s_fn = s_fp + 1
-    s_t = s_fn + 1
-    s_c = s_t + n_mer
-
-    def copy(src, dst, sec, out_no, in_no, mode, mer):
+    s_f, s_eo, s_ep, s_en, s_fp, s_fn, s_t, s_c = range(8)
+
+    def copy(src, dst, sec, no, mode, mer):
         return pltpu.make_async_remote_copy(
             src_ref=src,
             dst_ref=dst,
-            send_sem=send_sem.at[sec, out_no],
-            recv_sem=recv_sem.at[sec, in_no],
+            send_sem=send_sem.at[sec, no],
+            recv_sem=recv_sem.at[sec, no],
             device_id=at(mode, mer),
             device_id_type=MESH,
         )
 
     def f_copies(sec):
         return [
-            copy(f_part.at[sec, other_mode(k)], f_got.at[sec, me], sec, s_f + other_mode(k), s_f + me, other_mode(k), d)
+            copy(f_part.at[sec, other_mode(k)], f_got.at[sec, me], sec, s_f, other_mode(k), d)
             for k in range(1, n_mode)
         ]
 
     def t_copies(sec):
         return [
-            copy(t_part.at[sec], t_got.at[sec, d], sec, s_t + other_mer(k), s_t + d, me, other_mer(k))
+            copy(t_part.at[sec], t_got.at[sec, d], sec, s_t, me, other_mer(k))
             for k in range(1, n_mer)
         ]
 
     def up_copies(sec):
-        made = [copy(f_full.at[sec], f_prev.at[sec], sec, s_fp, s_fp, me, d + 1)]
+        made = [copy(f_full.at[sec], f_prev.at[sec], sec, s_fp, me, d + 1)]
         if sec == 0:
-            made.append(copy(connect_ref, c_prev, sec, s_c, s_c, me, d + 1))
+            made.append(copy(connect_ref, c_prev, sec, s_c, me, d + 1))
         return made
 
     def down_copies(sec):
-        return [copy(f_full.at[sec, :, pl.ds(0, GHOST)], f_next.at[sec], sec, s_fn, s_fn, me, d - 1)]
+        return [copy(f_full.at[sec, :, pl.ds(0, GHOST)], f_next.at[sec], sec, s_fn, me, d - 1)]
 
     def e_copies(sec):
         return [
-            copy(e_part.at[sec, other_mode(k)], e_own.at[sec, me], sec, s_eo + other_mode(k), s_eo + me, other_mode(k), d)
+            copy(e_part.at[sec, other_mode(k)], e_own.at[sec, me], sec, s_eo, other_mode(k), d)
             for k in range(1, n_mode)
         ]
 
     def e_up_copies(sec):
         return [
-            copy(e_part.at[sec, other_mode(k)], e_prev.at[sec, me], sec, s_ep + other_mode(k), s_ep + me, other_mode(k), d + 1)
+            copy(e_part.at[sec, other_mode(k)], e_prev.at[sec, me], sec, s_ep, other_mode(k), d + 1)
             for k in range(n_mode)
         ]
 
     def e_down_copies(sec):
         return [
-            copy(e_part.at[sec, other_mode(k)], e_next.at[sec, me], sec, s_en + other_mode(k), s_en + me, other_mode(k), d - 1)
+            copy(e_part.at[sec, other_mode(k)], e_next.at[sec, me], sec, s_en, other_mode(k), d - 1)
             for k in range(n_mode)
         ]
 
@@ -224,12 +217,14 @@
         for c in copies:
             c.start()
 
-    def sent(copies):
-        for c in copies:
-            c.wait_send()
+    def sent(ref, sec, no):
+        copy(ref, ref, sec, no, me, d).wait_send()
 
     def arrive(ref, sec, no):
-        copy(ref, ref, sec, no, no, me, d).wait_recv()
+        copy(ref, ref, sec, no, me, d).wait_recv()
+
+    most = pl.ds(0, n_mode - 1)
+    others = pl.ds(0, n_mer - 1)
 
     halves = 128 // wall_dev
 
@@ -322,7 +317,7 @@
 
         fill_pick(1, c_prev)
 
-    for load in loads[5:]:
+    for load in loads[5:8] + loads[9:]:
         load.wait()
     mass_inv = 1.0 / mass_ref[...]
     mode_no = me * mode_dev + lax.rem(iota((rows, 1), 0), mode_dev)
@@ -345,34 +340,35 @@
 
     def scatter(parts):
         low = [x.astype(BF) for x in parts]
-        total = mm_t(jnp.concatenate(low[:groups], 1), pick[0, :nodes, :])
-        extra = mm_t(jnp.concatenate(low[groups:], 1), pick[1, nodes:, :])
-        return jnp.concatenate([total[:, :GHOST] + extra, total[:, GHOST:]], 1)
+        total = mm_t(pick[0, :nodes, :], jnp.concatenate(low[:groups], 1))
+        extra = mm_t(pick[1, nodes:, :], jnp.concatenate(low[groups:], 1))
+        return jnp.concatenate([total[:GHOST] + extra, total[GHOST:]], 0).T
 
     def lanes(ref, sec, count):
         return jnp.concatenate([ref[sec, j] for j in range(count)], 1)
 
     def all_sent(sec):
-        sent(f_copies(sec))
-        sent(t_copies(sec))
-        sent(e_copies(sec))
+        sent(f_part.at[sec, most], sec, s_f)
+        sent(t_got.at[sec, others], sec, s_t)
+        sent(e_part.at[sec, most], sec, s_eo)
 
         @pl.when(has_next)
         def _():
-            sent(up_copies(sec))
-            sent(e_up_copies(sec))
+            sent(f_full.at[sec], sec, s_fp)
+            if sec == 0:
+                sent(connect_ref, sec, s_c)
+            sent(e_part.at[sec], sec, s_ep)
 
         @pl.when(has_prev)
         def _():
-            sent(down_copies(sec))
+            sent(f_next.at[sec], sec, s_fn)
 
         @pl.when(sends_down)
         def _():
-            sent(e_down_copies(sec))
+            sent(e_part.at[sec], sec, s_en)
 
     def rate(sec, value):
-        for k in range(1, n_mode):
-            arrive(f_got.at[sec, other_mode(k)], sec, s_f + other_mode(k))
+        arrive(f_got.at[sec, most], sec, s_f)
         phys = mm(forward_ref[...].astype(BF), f_got[sec].reshape(n_mode * rows, chunk))
         px, py, pz = [phys[c * nphi : (c + 1) * nphi] for c in range(3)]
         vx, vy, vz = [vel_ref[c].astype(F32) for c in range(3)]
@@ -392,6 +388,7 @@
 
         if sec == 0:
             prepare()
+            loads[8].wait()
         else:
             all_sent(0)
 
@@ -406,36 +403,32 @@
         here, back = gather_own(f_full[sec])
         diffused = elements(here + gather_next(f_next[sec]), back + gather_prev(f_prev[sec]), 0)
 
-        for k in range(1, n_mer):
-            arrive(t_got.at[sec, other_mer(k)], sec, s_t + other_mer(k))
+        arrive(t_got.at[sec, others], sec, s_t)
         trace = jnp.concatenate(
             [sum([t_got[sec, i + h] for h in range(1, halves)], t_got[sec, i]) for i in range(0, n_mer, halves)], 1
         )
-        wide = mm_t(trace, dtn_ref[...].reshape(mode_dev * wall_dev, trace.shape[1]))
+        wide = mm_t(dtn_ref[...].reshape(mode_dev * wall_dev, trace.shape[1]), trace).T
         wide = jnp.where(iota(wide.shape, 1) // wall_dev == lax.rem(iota(wide.shape, 0), mode_dev), wide, 0.0)
         folded = sum([wide[:, i : i + 128] for i in range(128, wide.shape[1], 128)], wide[:, :128])
         flux = sum([folded[:, h * wall_dev : (h + 1) * wall_dev] for h in range(1, halves)], folded[:, :wall_dev])
         for m in range(mode_dev):
             flux_ref[sec, m] = jnp.concatenate([flux[m : m + 1], flux[mode_dev + m : mode_dev + m + 1]], 0)
-        spots = mm_t(jnp.concatenate([-0.5 * flux] * halves, 1).astype(BF), wall_hot[...])
+        spots = mm_t(wall_hot[...], jnp.concatenate([-0.5 * flux] * halves, 1).astype(BF)).T
         blank = jnp.zeros((2 * mode_dev, nodes), F32)
         pulled = jnp.concatenate([blank, spots[:mode_dev], blank, spots[mode_dev:]], 0)
 
-        for k in range(1, n_mode):
-            arrive(e_own.at[sec, other_mode(k)], sec, s_eo + other_mode(k))
+        arrive(e_own.at[sec, most], sec, s_eo)
         here, back = gather_own(lanes(e_own, sec, n_mode))
 
         @pl.when(has_prev)
         def _():
-            for j in range(n_mode):
-                arrive(e_prev.at[sec, j], sec, s_ep + j)
+            arrive(e_prev.at[sec], sec, s_ep)
 
         back = back + gather_prev(lanes(e_prev, sec, n_mode))
 
         @pl.when(has_next)
         def _():
-            for j in range(ghosts):
-                arrive(e_next.at[sec, j], sec, s_en + j)
+            arrive(e_next.at[sec], sec, s_en)
 
         here = here + gather_next(lanes(e_next, sec, ghosts))
         curled = elements(here, back, 1)
@@ -454,14 +447,16 @@
     all_sent(1)
 
 
-def finish(out_in, flux_in, out_ref, flux_ref, sem):
-    copies = [
-        pltpu.make_async_copy(out_in, out_ref, sem.at[0]),
-        pltpu.make_async_copy(flux_in, flux_ref, sem.at[1]),
-    ]
-    for c in copies:
+def finish(out_in, flux_in, out_ref, flux_ref, out_mid, flux_mid, sem):
+    routes = [(flux_in, flux_mid, flux_ref), (out_in, out_mid, out_ref)]
+    inward = [pltpu.make_async_copy(a, b, sem.at[i]) for i, (a, b, _) in enumerate(routes)]
+    outward = [pltpu.make_async_copy(b, c, sem.at[2 + i]) for i, (_, b, c) in enumerate(routes)]
+    for c in inward:
         c.start()
-    for c in copies:
+    for c, then in zip(inward, outward):
+        c.wait()
+        then.start()
+    for c in outward:
         c.wait()
 
 
@@ -477,7 +472,6 @@
     chunk = nodes // n_mode
     ghosts = GHOST // chunk
     forward, inverse = transforms(modes, mode_dev, nphi)
-    sems = 4 * n_mode + n_mer + 3
     vmem = pl.BlockSpec(memory_space=pltpu.VMEM)
     hbm = pl.BlockSpec(memory_space=pltpu.HBM)
     shapes = (
@@ -515,8 +509,8 @@
             pltpu.VMEM(dtn.shape, BF),
             pltpu.VMEM(forward.shape, F32),
             pltpu.VMEM(inverse.shape, F32),
-            pltpu.SemaphoreType.DMA((2, sems)),
-            pltpu.SemaphoreType.DMA((2, sems)),
+            pltpu.SemaphoreType.DMA((2, 8)),
+            pltpu.SemaphoreType.DMA((2, 8)),
             pltpu.SemaphoreType.DMA((10,)),
         ],
         compiler_params=pltpu.CompilerParams(
@@ -539,7 +533,11 @@
         out_shape=shapes,
         in_specs=[hbm] * 2,
         out_specs=(hbm, hbm),
-        scratch_shapes=[pltpu.SemaphoreType.DMA((2,))],
+        scratch_shapes=[
+            pltpu.VMEM(shapes[0].shape, F32),
+            pltpu.VMEM(shapes[1].shape, F32),
+            pltpu.SemaphoreType.DMA((4,)),
+        ],
         compiler_params=pltpu.CompilerParams(vmem_limit_bytes=60 * 1024 * 1024),
     )(advanced, flux)
     return jnp.swapaxes(advanced, 0, 1), flux

time: 29.3 us -> 26.8 us (0.915)
  Pallas kernels: 28.5 us -> 26 us
    pallas_call x1, Pallas kernels: 4.59 us -> 1.58 us  [body(): pl.pallas_call(finish, out_shape=shapes, in_specs=[hbm] * 2, out_specs=(h...]
    pallas_call x1, Pallas kernels: 23.9 us -> 24.4 us  [body(): pl.pallas_call(functools.partial(kernel, n_mode, n_mer, modes), out_shape...]
where the time goes in v5:
time: 26.8 us; the launch traced here: 26.6 us
  Pallas kernels  26 us (97%)
  between operations  0.64 us (2%)
    pallas_call x1, Pallas kernels, body(): pl.pallas_call(functools.partial(kernel, n_mode, n_mer, modes), out_shape...  24.4 us
    pallas_call x1, Pallas kernels, body(): pl.pallas_call(finish, out_shape=shapes, in_specs=[hbm] * 2, out_specs=(h...  1.58 us

profile of v5, /device:TPU:0, one launch (start us, length us, event | category | flops | bytes accessed | tf_op | source)
XLA Modules:
  0.0 26.6 jit_solution(17863454922551293051)
XLA Ops:
  0.6 24.4 %shard_map.113 = (f32[6,8,512]{2,1,0:T(8,128)}, f32[2,8,2,64]{3,2,1,0:T(2,128)}) custom-call(f32[6,8,512]{2,1,0:T(8,128)} %bitcast.4, bf16[3,64,128]{2,1,0:T(8,128)(2,1)} %vel_in.1, f32[64,64]{1,0:T(8,128)} %stiff_in.1, f32[64,64]{1,0:T(8,128)} %curl_in.1, f32[1,512]{1,0:T(1,128)} %bitcast.5, s32[16,64]{1,0:T(8,128)} %connect_in.1, s32[1,64]{1,0:T(1,128)} %bitcast.6, ...), custom_call_target="tpu_custom_call" | custom-call | tf_op jit(solution)/shard_map/pallas_call | solution.py:481
  25.0 1.6 %shard_map.114 = (f32[6,8,512]{2,1,0:T(8,128)}, f32[2,8,2,64]{3,2,1,0:T(2,128)}) custom-call(f32[6,8,512]{2,1,0:T(8,128)} %get-tuple-element.6.out_in, f32[2,8,2,64]{3,2,1,0:T(2,128)} %get-tuple-element.7.flux_in), custom_call_target="tpu_custom_call" | custom-call | tf_op jit(solution)/shard_map/pallas_call | solution.py:531

commit v6 on v5

--- a/solution.py
+++ b/solution.py
@@ -140,22 +140,8 @@
     for k in range(1, n_mode):
         greet(other_mode(k), d)
 
-    @pl.when(has_prev)
-    def _():
-        for k in range(n_mode):
-            greet(other_mode(k), d - 1)
-
-    @pl.when(has_next)
-    def _():
-        for k in range(n_mode):
-            greet(other_mode(k), d + 1)
-
     for k in range(1, n_mer):
-        peer = other_mer(k)
-
-        @pl.when(jnp.logical_and(peer != d - 1, peer != d + 1))
-        def _():
-            greet(me, peer)
+        greet(me, other_mer(k))
 
     for load in loads[1:]:
         load.start()
@@ -200,18 +186,10 @@
         ]
 
     def e_up_copies(sec):
-        return [
-            copy(e_part.at[sec, other_mode(k)], e_prev.at[sec, me], sec, s_ep, other_mode(k), d + 1)
-            for k in range(n_mode)
-        ]
+        return [copy(e_own.at[sec], e_prev.at[sec], sec, s_ep, me, d + 1)]
 
     def e_down_copies(sec):
-        return [
-            copy(e_part.at[sec, other_mode(k)], e_next.at[sec, me], sec, s_en, other_mode(k), d - 1)
-            for k in range(n_mode)
-        ]
-
-    sends_down = jnp.logical_and(has_prev, me < ghosts)
+        return [copy(e_own.at[sec, pl.ds(0, ghosts)], e_next.at[sec], sec, s_en, me, d - 1)]
 
     def start(copies):
         for c in copies:
@@ -268,9 +246,7 @@
         f_next[...] = jnp.zeros(f_next.shape, BF)
         e_next[...] = jnp.zeros(e_next.shape, BF)
 
-    prev_n = has_prev.astype(jnp.int32)
-    next_n = has_next.astype(jnp.int32)
-    pl.semaphore_wait(barrier, n_mode - 1 + n_mer - 1 + (n_mode - 1) * (prev_n + next_n))
+    pl.semaphore_wait(barrier, n_mode - 1 + n_mer - 1)
 
     loads[1].wait()
     send_field(0)
@@ -340,9 +316,9 @@
 
     def scatter(parts):
         low = [x.astype(BF) for x in parts]
-        total = mm_t(pick[0, :nodes, :], jnp.concatenate(low[:groups], 1))
-        extra = mm_t(pick[1, nodes:, :], jnp.concatenate(low[groups:], 1))
-        return jnp.concatenate([total[:GHOST] + extra, total[GHOST:]], 0).T
+        total = mm_t(jnp.concatenate(low[:groups], 1), pick[0, :nodes, :])
+        extra = mm_t(jnp.concatenate(low[groups:], 1), pick[1, nodes:, :])
+        return jnp.concatenate([total[:, :GHOST] + extra, total[:, GHOST:]], 1)
 
     def lanes(ref, sec, count):
         return jnp.concatenate([ref[sec, j] for j in range(count)], 1)
@@ -357,15 +333,12 @@
             sent(f_full.at[sec], sec, s_fp)
             if sec == 0:
                 sent(connect_ref, sec, s_c)
-            sent(e_part.at[sec], sec, s_ep)
+            sent(e_own.at[sec], sec, s_ep)
 
         @pl.when(has_prev)
         def _():
             sent(f_next.at[sec], sec, s_fn)
-
-        @pl.when(sends_down)
-        def _():
-            sent(e_part.at[sec], sec, s_en)
+            sent(e_next.at[sec], sec, s_en)
 
     def rate(sec, value):
         arrive(f_got.at[sec, most], sec, s_f)
@@ -378,14 +351,6 @@
         e_own[sec, me] = e_part[sec, me]
         start(e_copies(sec))
 
-        @pl.when(has_next)
-        def _():
-            start(e_up_copies(sec))
-
-        @pl.when(sends_down)
-        def _():
-            start(e_down_copies(sec))
-
         if sec == 0:
             prepare()
             loads[8].wait()
@@ -407,17 +372,26 @@
         trace = jnp.concatenate(
             [sum([t_got[sec, i + h] for h in range(1, halves)], t_got[sec, i]) for i in range(0, n_mer, halves)], 1
         )
-        wide = mm_t(dtn_ref[...].reshape(mode_dev * wall_dev, trace.shape[1]), trace).T
+        wide = mm_t(trace, dtn_ref[...].reshape(mode_dev * wall_dev, trace.shape[1]))
         wide = jnp.where(iota(wide.shape, 1) // wall_dev == lax.rem(iota(wide.shape, 0), mode_dev), wide, 0.0)
         folded = sum([wide[:, i : i + 128] for i in range(128, wide.shape[1], 128)], wide[:, :128])
         flux = sum([folded[:, h * wall_dev : (h + 1) * wall_dev] for h in range(1, halves)], folded[:, :wall_dev])
         for m in range(mode_dev):
             flux_ref[sec, m] = jnp.concatenate([flux[m : m + 1], flux[mode_dev + m : mode_dev + m + 1]], 0)
-        spots = mm_t(wall_hot[...], jnp.concatenate([-0.5 * flux] * halves, 1).astype(BF)).T
+        spots = mm_t(jnp.concatenate([-0.5 * flux] * halves, 1).astype(BF), wall_hot[...])
         blank = jnp.zeros((2 * mode_dev, nodes), F32)
         pulled = jnp.concatenate([blank, spots[:mode_dev], blank, spots[mode_dev:]], 0)
 
         arrive(e_own.at[sec, most], sec, s_eo)
+
+        @pl.when(has_next)
+        def _():
+            start(e_up_copies(sec))
+
+        @pl.when(has_prev)
+        def _():
+            start(e_down_copies(sec))
+
         here, back = gather_own(lanes(e_own, sec, n_mode))
 
         @pl.when(has_prev)

time: 26.8 us -> 28.8 us (1.075)
  the two profiles are of different devices: /device:TPU:0 before, /device:TPU:1 now
where the time goes in v6:
time: 28.8 us; the launch traced here: 28.5 us
  Pallas kernels  27.9 us (97%)
  between operations  0.64 us (2%)
    pallas_call x1, Pallas kernels, body(): pl.pallas_call(functools.partial(kernel, n_mode, n_mer, modes), out_shape...  26.3 us
    pallas_call x1, Pallas kernels, body(): pl.pallas_call(finish, out_shape=shapes, in_specs=[hbm] * 2, out_specs=(h...  1.58 us

profile of v6, /device:TPU:1, one launch (start us, length us, event | category | flops | bytes accessed | tf_op | source)
XLA Modules:
  0.0 28.5 jit_solution(1035805280170809654)
XLA Ops:
  0.6 26.3 %shard_map.113 = (f32[6,8,512]{2,1,0:T(8,128)}, f32[2,8,2,64]{3,2,1,0:T(2,128)}) custom-call(f32[6,8,512]{2,1,0:T(8,128)} %bitcast.4, bf16[3,64,128]{2,1,0:T(8,128)(2,1)} %vel_in.1, f32[64,64]{1,0:T(8,128)} %stiff_in.1, f32[64,64]{1,0:T(8,128)} %curl_in.1, f32[1,512]{1,0:T(1,128)} %bitcast.5, s32[16,64]{1,0:T(8,128)} %connect_in.1, s32[1,64]{1,0:T(1,128)} %bitcast.6, ...), custom_call_target="tpu_custom_call" | custom-call | tf_op jit(solution)/shard_map/pallas_call | solution.py:455
  26.9 1.6 %shard_map.114 = (f32[6,8,512]{2,1,0:T(8,128)}, f32[2,8,2,64]{3,2,1,0:T(2,128)}) custom-call(f32[6,8,512]{2,1,0:T(8,128)} %get-tuple-element.6.out_in, f32[2,8,2,64]{3,2,1,0:T(2,128)} %get-tuple-element.7.flux_in), custom_call_target="tpu_custom_call" | custom-call | tf_op jit(solution)/shard_map/pallas_call | solution.py:505

commit v7 on v2

--- a/solution.py
+++ b/solution.py
@@ -436,6 +436,19 @@
             sent(e_down_copies(sec))
 
 
+def finish(out_in, flux_in, out_ref, flux_ref, out_mid, flux_mid, sem):
+    routes = [(flux_in, flux_mid, flux_ref), (out_in, out_mid, out_ref)]
+    inward = [pltpu.make_async_copy(a, b, sem.at[i]) for i, (a, b, _) in enumerate(routes)]
+    outward = [pltpu.make_async_copy(b, c, sem.at[2 + i]) for i, (_, b, c) in enumerate(routes)]
+    for c in inward:
+        c.start()
+    for c, then in zip(inward, outward):
+        c.wait()
+        then.start()
+    for c in outward:
+        c.wait()
+
+
 def body(field, velocity, stiffness, curl_matrix, mass, connect, wall_index, dtn):
     n_mode = lax.axis_size("mode")
     n_mer = lax.axis_size("mer")
@@ -451,12 +464,13 @@
     sems = 4 * n_mode + n_mer + 3
     vmem = pl.BlockSpec(memory_space=pltpu.VMEM)
     hbm = pl.BlockSpec(memory_space=pltpu.HBM)
+    shapes = (
+        jax.ShapeDtypeStruct((6, mode_dev, nodes), F32),
+        jax.ShapeDtypeStruct((2, mode_dev, 2, wall_dev), F32),
+    )
     advanced, flux = pl.pallas_call(
         functools.partial(kernel, n_mode, n_mer, modes),
-        out_shape=(
-            jax.ShapeDtypeStruct((6, mode_dev, nodes), F32),
-            jax.ShapeDtypeStruct((2, mode_dev, 2, wall_dev), F32),
-        ),
+        out_shape=shapes,
         in_specs=[hbm] * 10,
         out_specs=(vmem, vmem),
         scratch_shapes=[
@@ -504,6 +518,18 @@
         forward,
         inverse,
     )
+    advanced, flux = pl.pallas_call(
+        finish,
+        out_shape=shapes,
+        in_specs=[hbm] * 2,
+        out_specs=(hbm, hbm),
+        scratch_shapes=[
+            pltpu.VMEM(shapes[0].shape, F32),
+            pltpu.VMEM(shapes[1].shape, F32),
+            pltpu.SemaphoreType.DMA((4,)),
+        ],
+        compiler_params=pltpu.CompilerParams(vmem_limit_bytes=60 * 1024 * 1024),
+    )(advanced, flux)
     return jnp.swapaxes(advanced, 0, 1), flux
 
 

time: 26.6 us -> 26.1 us (0.981)
  local copies, waits for them, and re-layouts: 2.15 us -> 0 us
  Pallas kernels: 23.5 us -> 25.1 us
    unnamed x4 -> x0, local copies, waits for them, and re-layouts: 2.15 us -> none
    pallas_call x0 -> x1, Pallas kernels: none -> 1.58 us  [body(): pl.pallas_call(finish, out_shape=shapes, in_specs=[hbm] * 2, out_specs=(h...]
where the time goes in v7:
time: 26.1 us; the launch traced here: 25.8 us
  Pallas kernels  25.1 us (96%)
  between operations  0.64 us (2%)
    pallas_call x1, Pallas kernels, body(): pl.pallas_call(functools.partial(kernel, n_mode, n_mer, modes), out_shape...  23.5 us
    pallas_call x1, Pallas kernels, body(): pl.pallas_call(finish, out_shape=shapes, in_specs=[hbm] * 2, out_specs=(h...  1.58 us

profile of v7, /device:TPU:0, one launch (start us, length us, event | category | flops | bytes accessed | tf_op | source)
XLA Modules:
  0.0 25.8 jit_solution(13130906115532984078)
XLA Ops:
  0.6 23.5 %shard_map.113 = (f32[6,8,512]{2,1,0:T(8,128)}, f32[2,8,2,64]{3,2,1,0:T(2,128)}) custom-call(f32[6,8,512]{2,1,0:T(8,128)} %bitcast.4, bf16[3,64,128]{2,1,0:T(8,128)(2,1)} %vel_in.1, f32[64,64]{1,0:T(8,128)} %stiff_in.1, f32[64,64]{1,0:T(8,128)} %curl_in.1, f32[1,512]{1,0:T(1,128)} %bitcast.5, s32[16,64]{1,0:T(8,128)} %connect_in.1, s32[1,64]{1,0:T(1,128)} %bitcast.6, ...), custom_call_target="tpu_custom_call" | custom-call | tf_op jit(solution)/shard_map/pallas_call | solution.py:471
  24.2 1.6 %shard_map.114 = (f32[6,8,512]{2,1,0:T(8,128)}, f32[2,8,2,64]{3,2,1,0:T(2,128)}) custom-call(f32[6,8,512]{2,1,0:T(8,128)} %get-tuple-element.6.out_in, f32[2,8,2,64]{3,2,1,0:T(2,128)} %get-tuple-element.7.flux_in), custom_call_target="tpu_custom_call" | custom-call | tf_op jit(solution)/shard_map/pallas_call | solution.py:521
